TPU v7x, 256 devices: a whole 4x4x8 slice. The times are simulated.
256 devices in a mesh: row: 16 (over z_lo, x, core), col: 16 (over y, z_hi).
Axes of the slice: x: 4, y: 4, z: 8 (z_hi: 4, z_lo: 2; z = z_hi * 2 + z_lo), core: 2. Of those that a mesh axis runs over, the one named last changes fastest.
Arguments:
- embeddings: bfloat16 [384, 65536], P(None, ('row', 'col')), may hold values from -6 to 6
- solution: float32 [16, 65536], P(None, ('row', 'col')), may hold values from -6 to 6
- residual: float32 [16, 65536], P(None, ('row', 'col')), may hold values from -6 to 6
- direction: float32 [16, 65536], P(None, ('row', 'col')), may hold values from -6 to 6
Outputs:
- solution_next: float32 [16, 65536], P(None, ('row', 'col'))
- residual_next: float32 [16, 65536], P(None, ('row', 'col'))
- direction_next: float32 [16, 65536], P(None, ('row', 'col'))
All inputs are finite; a program needn't handle non-finite values.
Results may differ from a plain program's by a relative error of at most 0.0003.
Values may be sent and summed in bfloat16 or wider, within the bound.
A program may use at most 64 MiB of HBM per device.

v0:
```python
import math

import jax
import jax.numpy as jnp
from jax import lax
from jax.sharding import PartitionSpec as P

ridge_weight = 0.5
highest = lax.Precision.HIGHEST


def column_squares(values):
    floats = values.astype(jnp.float32)
    return jnp.sum(floats * floats, axis=0)


def spd_solve(matrix, right):
    factor = jnp.linalg.cholesky(matrix)
    middle = lax.linalg.triangular_solve(factor, right, left_side=True, lower=True)
    return lax.linalg.triangular_solve(factor, middle, left_side=True, lower=True, transpose_a=True)


def kernel_block(row_piece, row_norms, col_piece, col_norms):
    feature_width = row_piece.shape[0]
    cross = jnp.dot(col_piece.T, row_piece, preferred_element_type=jnp.float32)
    distance = col_norms[:, None] + row_norms[None, :] - 2.0 * cross
    return jnp.exp(distance * (-2.0 / feature_width))


def kernel_apply(row_points, row_sq, col_points, col_sq, col_weights):
    row_count = row_points.shape[1]
    col_count = col_points.shape[1]
    row_span = math.gcd(row_count, 512)
    col_span = math.gcd(col_count, 512)
    rubric_count = col_weights.shape[0]

    def row_step(index_row, running):
        row_piece = lax.dynamic_slice_in_dim(row_points, index_row * row_span, row_span, 1)
        row_norms = lax.dynamic_slice_in_dim(row_sq, index_row * row_span, row_span, 0)

        def col_step(index_col, partial_value):
            col_piece = lax.dynamic_slice_in_dim(col_points, index_col * col_span, col_span, 1)
            col_norms = lax.dynamic_slice_in_dim(col_sq, index_col * col_span, col_span, 0)
            col_part = lax.dynamic_slice_in_dim(col_weights, index_col * col_span, col_span, 1)
            kernel = kernel_block(row_piece, row_norms, col_piece, col_norms)
            return partial_value + jnp.dot(col_part, kernel, precision=highest)

        partial_value = lax.fori_loop(
            0, col_count // col_span, col_step, jnp.zeros((rubric_count, row_span), jnp.float32)
        )
        return lax.dynamic_update_slice_in_dim(running, partial_value, index_row * row_span, 1)

    return lax.fori_loop(
        0, row_count // row_span, row_step, jnp.zeros((rubric_count, row_count), jnp.float32)
    )


def shards(embeddings, solution, residual, direction):
    row_points = lax.all_gather(embeddings, "col", axis=1, tiled=True)
    row_sq = column_squares(row_points)
    col_points = lax.all_gather(embeddings.astype(jnp.float32), "row", axis=1, tiled=True).astype(
        jnp.bfloat16
    )
    col_weights = lax.all_gather(direction, "row", axis=1, tiled=True)
    applied = kernel_apply(row_points, row_sq, col_points, column_squares(col_points), col_weights)
    product = (
        lax.psum_scatter(applied, "col", scatter_dimension=1, tiled=True) + ridge_weight * direction
    )
    local_curv = jnp.dot(direction, product.T, precision=highest)
    local_old = jnp.dot(residual, residual.T, precision=highest)
    curvature, old_gram = lax.psum((local_curv, local_old), ("row", "col"))
    curvature = 0.5 * (curvature + curvature.T)
    alpha_mat = spd_solve(curvature, old_gram)
    residual_next = residual - jnp.dot(alpha_mat.T, product, precision=highest)
    new_gram = lax.psum(jnp.dot(residual_next, residual_next.T, precision=highest), ("row", "col"))
    solution_next = solution + jnp.dot(alpha_mat.T, direction, precision=highest)
    beta_mat = spd_solve(old_gram, new_gram)
    direction_next = residual_next + jnp.dot(beta_mat.T, direction, precision=highest)
    return (solution_next, residual_next, direction_next)


def solution(mesh):
    return jax.shard_map(
        shards,
        mesh=mesh,
        in_specs=(
            P(None, ("row", "col")),
            P(None, ("row", "col")),
            P(None, ("row", "col")),
            P(None, ("row", "col")),
        ),
        out_specs=(P(None, ("row", "col")), P(None, ("row", "col")), P(None, ("row", "col"))),
        check_vma=False,
    )
```

profile of v0, /device:TPU:1, one launch (start us, length us, event | category | flops | bytes accessed | tf_op | source)
XLA Modules:
  0.0 539.8 jit_solution(3119237399278504860)
XLA Ops:
  8.7 22.4 %all_gather.10 = f32[16,4096]{1,0:T(8,128)S(1)} all-gather(f32[16,256]{1,0:T(8,128)} %param.16), channel_id=1, replica_groups=mesh['row'=16,'col'=16] {'row'}, dimensions={1}, use_global_device_ids=true | all-gather | bytes 278528 | tf_op jit(solution)/shard_map/all_gather | solution.py:64
  31.1 27.6 %all-gather.5.cloned.1.call-done = bf16[384,4096]{1,0:T(8,128)(2,1)} async-done(((bf16[384,256]{1,0:T(8,128)(2,1)}), bf16[384,4096]{1,0:T(8,128)(2,1)}) %all-gather.5.cloned.1.call-update) | async-done | bytes 3145744 | tf_op jit(solution)/shard_map/all_gather | solution.py:61
  58.7 2.6 multiply_reduce_fusion
  61.3 71.1 %all-gather.3.cloned.1.call-done = bf16[384,4096]{1,0:T(8,128)(2,1)} async-done(((bf16[384,256]{1,0:T(8,128)(2,1)}), bf16[384,4096]{1,0:T(8,128)(2,1)}) %all-gather.3.cloned.1.call-update) | async-done | bytes 3145744 | tf_op jit(solution)/shard_map/all_gather | solution.py:59
  132.5 2.6 multiply_reduce_fusion.1
  135.1 153.1 %while.40 = (s32[]{:T(128)}, f32[16,4096]{1,0:T(8,128)S(1)}, bf16[384,4096]{1,0:T(8,128)(2,1)}, f32[4096]{0:T(1024)S(1)}, f32[16,4096]{1,0:T(8,128)S(1)}, /*inde...) while((s32[]{:T(128)}, f32[16,4096]{1,0:T(8,128)S(1)}, ...), condition=%wide.region_5.0_spmd, body=%wide.region_2.0_spmd.sunk | while | flops 252723200 | bytes 3846616 | solution.py:53
  136.2 18.0 %while.41 = (s32[]{:T(128)}, f32[16,512]{1,0:T(8,128)S(1)}, f32[16,4096]{1,0:T(8,128)S(1)}, f32[4096]{0:T(1024)S(1)}, f32[512]{0:T(512)S(1)}, /*index=5*/bf16[38...) while((s32[]{:T(128)}, f32[16,512]{1,0:T(8,128)S(1)}, ...), condition=%wide.region_4.0_spmd.clone, body=%wide.region_3.0_spmd.clone.sunk | while | flops 252723200 | bytes 2990257 | solution.py:48
  136.3 1.5 fusion.51
  155.4 18.0 %while.41 = (s32[]{:T(128)}, f32[16,512]{1,0:T(8,128)S(1)}, f32[16,4096]{1,0:T(8,128)S(1)}, f32[4096]{0:T(1024)S(1)}, f32[512]{0:T(512)S(1)}, /*index=5*/bf16[38...) while((s32[]{:T(128)}, f32[16,512]{1,0:T(8,128)S(1)}, ...), condition=%wide.region_4.0_spmd.clone, body=%wide.region_3.0_spmd.clone.sunk | while | flops 252723200 | bytes 2990257 | solution.py:48
  157.7 1.5 fusion.51
  174.5 18.0 %while.41 = (s32[]{:T(128)}, f32[16,512]{1,0:T(8,128)S(1)}, f32[16,4096]{1,0:T(8,128)S(1)}, f32[4096]{0:T(1024)S(1)}, f32[512]{0:T(512)S(1)}, /*index=5*/bf16[38...) while((s32[]{:T(128)}, f32[16,512]{1,0:T(8,128)S(1)}, ...), condition=%wide.region_4.0_spmd.clone, body=%wide.region_3.0_spmd.clone.sunk | while | flops 252723200 | bytes 2990257 | solution.py:48
  174.6 1.5 fusion.51
  193.6 18.0 %while.41 = (s32[]{:T(128)}, f32[16,512]{1,0:T(8,128)S(1)}, f32[16,4096]{1,0:T(8,128)S(1)}, f32[4096]{0:T(1024)S(1)}, f32[512]{0:T(512)S(1)}, /*index=5*/bf16[38...) while((s32[]{:T(128)}, f32[16,512]{1,0:T(8,128)S(1)}, ...), condition=%wide.region_4.0_spmd.clone, body=%wide.region_3.0_spmd.clone.sunk | while | flops 252723200 | bytes 2990257 | solution.py:48
  212.7 18.0 %while.41 = (s32[]{:T(128)}, f32[16,512]{1,0:T(8,128)S(1)}, f32[16,4096]{1,0:T(8,128)S(1)}, f32[4096]{0:T(1024)S(1)}, f32[512]{0:T(512)S(1)}, /*index=5*/bf16[38...) while((s32[]{:T(128)}, f32[16,512]{1,0:T(8,128)S(1)}, ...), condition=%wide.region_4.0_spmd.clone, body=%wide.region_3.0_spmd.clone.sunk | while | flops 252723200 | bytes 2990257 | solution.py:48
  212.8 1.5 fusion.51
  231.9 18.0 %while.41 = (s32[]{:T(128)}, f32[16,512]{1,0:T(8,128)S(1)}, f32[16,4096]{1,0:T(8,128)S(1)}, f32[4096]{0:T(1024)S(1)}, f32[512]{0:T(512)S(1)}, /*index=5*/bf16[38...) while((s32[]{:T(128)}, f32[16,512]{1,0:T(8,128)S(1)}, ...), condition=%wide.region_4.0_spmd.clone, body=%wide.region_3.0_spmd.clone.sunk | while | flops 252723200 | bytes 2990257 | solution.py:48
  232.0 1.5 fusion.51
  251.0 18.0 %while.41 = (s32[]{:T(128)}, f32[16,512]{1,0:T(8,128)S(1)}, f32[16,4096]{1,0:T(8,128)S(1)}, f32[4096]{0:T(1024)S(1)}, f32[512]{0:T(512)S(1)}, /*index=5*/bf16[38...) while((s32[]{:T(128)}, f32[16,512]{1,0:T(8,128)S(1)}, ...), condition=%wide.region_4.0_spmd.clone, body=%wide.region_3.0_spmd.clone.sunk | while | flops 252723200 | bytes 2990257 | solution.py:48
  251.1 1.5 fusion.51
  270.1 18.0 %while.41 = (s32[]{:T(128)}, f32[16,512]{1,0:T(8,128)S(1)}, f32[16,4096]{1,0:T(8,128)S(1)}, f32[4096]{0:T(1024)S(1)}, f32[512]{0:T(512)S(1)}, /*index=5*/bf16[38...) while((s32[]{:T(128)}, f32[16,512]{1,0:T(8,128)S(1)}, ...), condition=%wide.region_4.0_spmd.clone, body=%wide.region_3.0_spmd.clone.sunk | while | flops 252723200 | bytes 2990257 | solution.py:48
  270.2 1.5 fusion.51
  289.0 82.3 %reduce-scatter.2.cloned.1.call-done = f32[16,256]{1,0:T(8,128)} async-done(((f32[16,4096]{1,0:T(8,128)}), f32[16,256]{1,0:T(8,128)}) %reduce-scatter.2.cloned.1.call-update) | async-done | bytes 16400 | tf_op jit(solution)/shard_map/reduce_scatter | solution.py:67
  372.2 75.8 %all-reduce = (f32[16,16]{0,1:T(8,128)S(1)}, f32[16,16]{1,0:T(8,128)S(1)}) all-reduce(f32[16,16]{0,1:T(8,128)S(1)} %fusion.24, f32[16,16]{1,0:T(8,128)S(1)} %convolution_bitcast_fusion), channel_id=1, replica_groups=mesh['row'=16,'col'=16] {'row','col'}, use_global_device_ids=true, to_apply=%region_10.12 | all-reduce | flops 512 | bytes 4096 | tf_op jit(solution)/shard_map/psum | solution.py:71
  453.7 73.6 %psum.23 = f32[16,16]{1,0:T(8,128)S(1)} all-reduce(f32[16,16]{1,0:T(8,128)S(1)} %fusion.25), channel_id=1, replica_groups=mesh['row'=16,'col'=16] {'row','col'}, use_global_device_ids=true, to_apply=%region_11.15 | all-reduce | flops 256 | bytes 2048 | tf_op jit(solution)/shard_map/psum | solution.py:75
  (260 shorter events, 156.0 us)
Async XLA Ops:
  7.2 51.6 %all-gather.5.cloned.1.call-start = ((), (), s32[]{:S(2)}) async-start(), calls=%async_computation.2 | async-start | bytes 3342336 | tf_op jit(solution)/shard_map/all_gather | solution.py:61
  7.9 124.6 %all-gather.3.cloned.1.call-start = ((), (), s32[]{:S(2)}) async-start(), calls=%async_computation.1 | async-start | bytes 3342336 | tf_op jit(solution)/shard_map/all_gather | solution.py:59
  8.6 362.7 %reduce-scatter.2.cloned.1.call-start = ((), (), s32[]{:S(2)}) async-start(), calls=%async_computation.3 | async-start | bytes 278528 | tf_op jit(solution)/shard_map/reduce_scatter | solution.py:67
  135.1 153.8 %copy-start.3 = (f32[16,256]{1,0:T(8,128)S(1)}, f32[16,256]{1,0:T(8,128)}, u32[]{:S(2)}) copy-start(f32[16,256]{1,0:T(8,128)} %param.15) | copy-start | bytes 49156
  135.1 236.3 %copy-start.1 = (f32[16,256]{1,0:T(8,128)S(1)}, f32[16,256]{1,0:T(8,128)}, u32[]{:S(2)}) copy-start(f32[16,256]{1,0:T(8,128)} %param.16) | copy-start | bytes 49156
  135.1 397.3 %copy-start.4 = (f32[16,256]{1,0:T(8,128)S(1)}, f32[16,256]{1,0:T(8,128)}, u32[]{:S(2)}) copy-start(f32[16,256]{1,0:T(8,128)} %param.14) | copy-start | bytes 49156
  288.2 0.7 copy-start
  453.5 79.7 %copy-start.2 = (f32[16,256]{1,0:T(8,128)}, f32[16,256]{1,0:T(8,128)S(1)}, u32[]{:S(2)}) copy-start(f32[16,256]{1,0:T(8,128)S(1)} %convolution_subtract_fusion) | copy-start | bytes 49156
Sparse Core Ops, SparseCore 0:
  9.8 48.9 all-gather.4
  61.1 71.2 all-gather.2
  289.0 82.3 reduce-scatter.1
where the time goes:
time: 543 us; the launch traced here: 540 us
  waiting for transfers between devices  182 us (34%)
  blocking collectives  172 us (32%)
  matrix products  143 us (26%)
  local copies, waits for them, and re-layouts  14.6 us (3%)
  between operations  13.8 us (3%)
  other arithmetic  13.2 us (2%)
    dot_general x64, matrix products, kernel_block(): cross = jnp.dot(col_piece.T, row_piece, preferred_element_type=jnp.float32)  98.4 us
    reduce_scatter x1, waiting for transfers between devices, shards(): lax.psum_scatter(applied, 'col', scatter_dimension=1, tiled=True)  82.3 us
    psum x1, blocking collectives, shards(): curvature, old_gram = lax.psum((local_curv, local_old), ('row', 'col'))  75.8 us
    psum x1, blocking collectives, shards(): lax.psum(jnp.dot(residual_next, residual_next.T, precision=highest), ('ro...  73.6 us
    all_gather x1, waiting for transfers between devices, shards(): row_points = lax.all_gather(embeddings, 'col', axis=1, tiled=True)  71.1 us
    dot_general x64, matrix products, col_step(): return partial_value + jnp.dot(col_part, kernel, precision=highest)  39.9 us
    all_gather x1, waiting for transfers between devices, shards(): lax.all_gather(embeddings.astype(jnp.float32), 'row', axis=1, tiled=True)  27.6 us
    all_gather x1, blocking collectives, shards(): col_weights = lax.all_gather(direction, 'row', axis=1, tiled=True)  22.4 us
  transfers between devices with their start and end apart: 3, of which 3 were waited for; matrix products, arithmetic and copies ran while one was open for 1% of the time, Pallas kernels for 0%

commit v1 on v0

v1 whole, which is shorter than its diff:
```python
import functools

import jax
import jax.numpy as jnp
from jax import lax
from jax.experimental import pallas as pl
from jax.experimental.pallas import tpu as pltpu
from jax.sharding import PartitionSpec as P

f32, bf16, f8 = jnp.float32, jnp.bfloat16, jnp.float8_e4m3fn
MESH = pl.DeviceIdType.MESH
highest = lax.Precision.HIGHEST

ridge_weight = 0.5
points = 256
rubrics = 16
width = 384
deep = 512
aug_at, hi_at, lo_at, rows_sent = 384, 400, 416, 432
low_scale, dir_scale, dir_step = 65536.0, 64.0, 16.0
scale = 4.0 / width

slots = [
    ((1, 0), (1, 0)),
    ((0, 3), (0, 3)),
    ((1, 3), (1, 0)),
    ((1, 1), (0, 1)),
    ((2, 1), (1, 0)),
    ((3, 2), (3, 0)),
    ((2, 0), (0, 3)),
    ((0, 2), (0, 3)),
    ((0, 0), None),
    ((2, 2), (0, 1)),
]
own = 8
place = {offset: index for index, (offset, _) in enumerate(slots)}
along_z = [0, 1, 7, 2, 6, 3, 5, 4]
half_rows = 208
tiles = 34


def parent(index):
    (ox, oy), (hx, hy) = slots[index]
    return place[((ox - hx) % 4, (oy - hy) % 4)]


def tile_at(t):
    late = t - 21
    i = jnp.where(t < 5, 0, 1)
    k = jnp.where(t < 5, t, t - 5)
    i = jnp.where(t >= 10, 2, i)
    k = jnp.where(t >= 10, t - 10, k)
    i = jnp.where(t >= 15, t - 15, i)
    k = jnp.where(t >= 15, 6, k)
    i = jnp.where(t >= 18, t - 18, i)
    k = jnp.where(t >= 18, 5, k)
    i = jnp.where(t >= 21, 3 + lax.rem(late, 2), i)
    k = jnp.where(t >= 21, jnp.maximum(2 * lax.div(late, 2) - 1, 0), k)
    i = jnp.where(t >= 29, t - 29, i)
    k = jnp.where(t >= 29, 7, k)
    last = t >= tiles
    return jnp.where(last, 0, i), jnp.where(last, 0, k)


def nt(left, right, precision=None):
    return lax.dot_general(
        left, right, (((1,), (1,)), ((), ())), precision=precision, preferred_element_type=f32
    )


def nn(left, right):
    return jnp.dot(left, right, precision=highest, preferred_element_type=f32)


def low_parts(pieces):
    whole = pieces.astype(f32)
    whole = (whole[:rubrics] + whole[rubrics:]) * dir_scale
    first = whole.astype(f8)
    second = ((whole - first.astype(f32)) * dir_step).astype(f8)
    return jnp.concatenate([first, second], axis=0)


def combine(parts):
    low = parts[32:48] + parts[48:64] * (1.0 / dir_step)
    return parts[0:16] + parts[16:32] + low * (1.0 / (low_scale * dir_scale))


def inverse(matrix):
    size = matrix.shape[0]
    row = lax.broadcasted_iota(jnp.int32, matrix.shape, 0)
    col = lax.broadcasted_iota(jnp.int32, matrix.shape, 1)
    for step in range(size):
        pivot_row = matrix[step : step + 1, :]
        pivot_col = matrix[:, step : step + 1]
        pivot = 1.0 / matrix[step : step + 1, step : step + 1]
        scaled = pivot_row * pivot
        inner = matrix - pivot_col * scaled
        at_row, at_col = row == step, col == step
        matrix = jnp.where(
            at_row,
            jnp.where(at_col, pivot, scaled),
            jnp.where(at_col, -pivot_col * pivot, inner),
        )
    return matrix


def kernel(
    e_ref, sol_ref, res_ref, dir_ref, sol_out, res_out, dir_out,
    xb, xa, la, acc_a, acc_b, s0, s1, part_a, part_b, sum_a, sum_b, gram, gram_xy, gram_zc,
    a_send, a_recv, z_send, z_recv, c_send, c_recv, pa_send, pa_recv, pb_send, pb_recv, g_send, g_recv,
):
    row, col = lax.axis_index("row"), lax.axis_index("col")
    core, x, z_lo = lax.rem(row, 2), lax.rem(lax.div(row, 2), 4), lax.div(row, 8)
    y, z_hi = lax.div(col, 4), lax.rem(col, 4)
    z = z_hi * 2 + z_lo

    def device(dx=0, dy=0, dz=0, dc=0):
        x2, y2 = lax.rem(x + dx % 4, 4), lax.rem(y + dy % 4, 4)
        z2, c2 = lax.rem(z + dz % 8, 8), lax.rem(core + dc, 2)
        return (lax.rem(z2, 2) * 8 + x2 * 2 + c2, y2 * 4 + lax.div(z2, 2))

    plane = [(o // 4, o % 4) for o in range(1, 16)]
    column = [(o // 2, o % 2) for o in range(1, 16)]

    barrier = pltpu.get_barrier_semaphore()
    for dx, dy in plane:
        pl.semaphore_signal(barrier, inc=1, device_id=device(dx=dx, dy=dy), device_id_type=MESH)
    for dz, dc in column:
        pl.semaphore_signal(barrier, inc=1, device_id=device(dz=dz, dc=dc), device_id_type=MESH)

    block = e_ref[...]
    wide = block.astype(f32)
    half = -0.5 * jnp.sum(wide * wide, axis=0, keepdims=True)
    h1 = half.astype(bf16).astype(f32)
    h2 = (half - h1).astype(bf16).astype(f32)
    h3 = half - h1 - h2
    at = lax.broadcasted_iota(jnp.int32, (16, points), 0)
    ones = jnp.where((at >= 8) & (at < 11), 1.0, 0.0)
    aug = jnp.where(at == 0, h1, jnp.where(at == 1, h2, jnp.where(at == 2, h3, ones)))
    way = dir_ref[...]
    way_hi = way.astype(bf16)
    way_lo = (way - way_hi.astype(f32)).astype(bf16)
    for buffer, slot in ((xb, 0), (xa, own)):
        buffer[slot, 0:width, :] = block
        buffer[slot, aug_at:hi_at, :] = aug.astype(bf16)
        buffer[slot, hi_at:lo_at, :] = way_hi
        buffer[slot, lo_at:rows_sent, :] = way_lo

    pl.semaphore_wait(barrier, 30)

    body_rows = pl.ds(0, rows_sent)

    def a_copy(index):
        hx, hy = slots[index][1]
        return pltpu.make_async_remote_copy(
            src_ref=xa.at[parent(index)], dst_ref=xa.at[index],
            send_sem=a_send.at[index], recv_sem=a_recv.at[index],
            device_id=device(dx=-hx, dy=-hy), device_id_type=MESH,
        )

    def z_copy(index):
        slot = min(index, 7)
        source = [None, 0, 0, 1, 2, 3, 4, 5, 6][index]
        rows = body_rows
        if index == 7:
            rows = pl.ds(0, half_rows)
        if index == 8:
            rows = pl.ds(half_rows, rows_sent - half_rows)
        step = -1 if index in (1, 3, 5, 7) else 1
        return pltpu.make_async_remote_copy(
            src_ref=xb.at[2 * source, rows, :], dst_ref=xb.at[2 * slot, rows, :],
            send_sem=z_send.at[index], recv_sem=z_recv.at[index],
            device_id=device(dz=step), device_id_type=MESH,
        )

    def c_copy(slot):
        return pltpu.make_async_remote_copy(
            src_ref=xb.at[2 * slot, body_rows, :], dst_ref=xb.at[2 * slot + 1, body_rows, :],
            send_sem=c_send.at[slot], recv_sem=c_recv.at[slot],
            device_id=device(dc=1), device_id_type=MESH,
        )

    def turn(index):
        rows = pl.ds(index * points, points)
        la[rows, 0:width] = xa[index, 0:width, :].T
        extra = xa[index, aug_at:hi_at, :].astype(f32)
        extra = jnp.concatenate([extra[8:16], extra[0:8], jnp.zeros((112, points), f32)], axis=0)
        la[rows, width:deep] = extra.T.astype(bf16)

    for index in (0, 1):
        a_copy(index).start()
    for index in (1, 2):
        z_copy(index).start()
    c_copy(0).start()

    turn(own)
    xb[:, rows_sent:deep, :] = jnp.zeros((16, deep - rows_sent, points), bf16)
    acc_a[...] = jnp.zeros_like(acc_a)
    acc_b[...] = jnp.zeros_like(acc_b)
    rest = res_ref[...]
    old = nt(rest, rest, highest)

    def cross(t, into):
        i, k = tile_at(t)
        left = la[pl.ds(pl.multiple_of(i * 512, 512), 512), :]
        into[:, 0:256] = jnp.dot(left, xb[2 * k], preferred_element_type=f32)
        into[:, 256:512] = jnp.dot(left, xb[2 * k + 1], preferred_element_type=f32)

    def consume(t, held):
        i, k = tile_at(t)
        weight = jnp.where((i >= 3) & ((k == 0) | (k == 7)), 0.5, 1.0).astype(f32)
        rows = pl.ds(pl.multiple_of(i * 512, 512), 512)
        values = jnp.exp(held[...] * scale)
        high = values.astype(bf16)
        low = ((values - high.astype(f32)) * low_scale).astype(f8)
        right = jnp.concatenate(
            [xb[2 * k, hi_at:rows_sent, :], xb[2 * k + 1, hi_at:rows_sent, :]], axis=1
        )
        acc_a[rows, 0:32] += nt(high, right) * weight
        acc_a[rows, 32:64] += nt(low, low_parts(right)) * weight
        left = jnp.concatenate(
            [xa[2 * i, hi_at:rows_sent, :], xa[2 * i + 1, hi_at:rows_sent, :]], axis=1
        )
        by_high = jnp.dot(left, high, preferred_element_type=f32) * weight
        by_low = jnp.dot(low_parts(left), low, preferred_element_type=f32) * weight
        for side in (0, 1):
            lanes = slice(side * 256, side * 256 + 256)
            acc_b[2 * k + side, 0:32, :] += by_high[:, lanes]
            acc_b[2 * k + side, 32:64, :] += by_low[:, lanes]

    def b_copy(slot):
        return pltpu.make_async_remote_copy(
            src_ref=part_b.at[slot], dst_ref=sum_b.at[slot],
            send_sem=pb_send.at[slot], recv_sem=pb_recv.at[slot],
            device_id=device(dz=along_z[slot // 2], dc=slot % 2), device_id_type=MESH,
        )

    def hand_back(*which):
        for k in which:
            for slot in (2 * k, 2 * k + 1):
                part_b[slot] = combine(acc_b[slot])
                if slot:
                    b_copy(slot).start()

    def first():
        for index in (0, 1):
            a_copy(index).wait_recv()
        for index in (1, 2):
            z_copy(index).wait_recv()
        for index in (2, 3, 7):
            a_copy(index).start()
        for index in (3, 4):
            z_copy(index).start()
        for slot in (1, 2):
            c_copy(slot).start()
        turn(0)
        turn(1)
        for slot in (0, 1, 2):
            c_copy(slot).wait_recv()

    def second():
        for index in (2, 3, 7):
            a_copy(index).wait_recv()
        for index in (3, 4):
            z_copy(index).wait_recv()
        for index in (4, 5):
            a_copy(index).start()
        for index in (5, 6):
            z_copy(index).start()
        for slot in (3, 4):
            c_copy(slot).start()
        for index in (2, 3, 7):
            turn(index)
        for slot in (3, 4):
            c_copy(slot).wait_recv()

    def third():
        for index in (4, 5):
            a_copy(index).wait_recv()
        for index in (5, 6):
            z_copy(index).wait_recv()
        for index in (6, 9):
            a_copy(index).start()
        for index in (7, 8):
            z_copy(index).start()
        for slot in (5, 6):
            c_copy(slot).start()
        for index in (4, 5):
            turn(index)
        for slot in (5, 6):
            c_copy(slot).wait_recv()

    def fourth():
        for index in (6, 9):
            a_copy(index).wait_recv()
        for index in (7, 8):
            z_copy(index).wait_recv()
        c_copy(7).start()
        for index in (6, 9):
            turn(index)
        c_copy(7).wait_recv()

    events = {1: second, 4: third, 10: fourth}
    ready = {8: (2, 4), 9: (6,), 12: (0,), 13: (1,), 14: (3,), 15: (5,)}
    for at_step, which in ready.items():
        events[at_step] = functools.partial(hand_back, *which)

    first()
    cross(jnp.int32(0), s0)

    def step(n, carry):
        for at_step, act in events.items():
            pl.when(n == at_step)(act)
        t = 2 * n
        cross(t + 1, s1)
        consume(t, s0)
        cross(t + 2, s0)
        consume(t + 1, s1)
        return carry

    lax.fori_loop(0, tiles // 2, step, 0)

    hand_back(7)

    def pa_copy(index):
        (ox, oy), _ = slots[index]
        return pltpu.make_async_remote_copy(
            src_ref=part_a.at[index], dst_ref=sum_a.at[index],
            send_sem=pa_send.at[index], recv_sem=pa_recv.at[index],
            device_id=device(dx=ox, dy=oy), device_id_type=MESH,
        )

    others = [index for index in range(10) if index != own]
    for index in others + [own]:
        part_a[index] = combine(acc_a[pl.ds(index * points, points), :].T)
        if index != own:
            pa_copy(index).start()

    product = part_a[own] + part_b[0] + ridge_weight * way
    for slot in range(1, 16):
        b_copy(slot).wait_recv()
        product = product + sum_b[slot]
    for index in others:
        pa_copy(index).wait_recv()
        product = product + sum_a[index]

    by_product = nt(jnp.concatenate([way, product, rest], axis=0), product, highest)
    of_product = nt(product, jnp.concatenate([way, rest], axis=0), highest)
    gram[0] = jnp.concatenate(
        [
            0.5 * (by_product[0:16] + of_product[:, 0:16]),
            of_product[:, 16:32],
            by_product[16:32],
            old,
            by_product[32:48],
            jnp.zeros((rubrics, 48), f32),
        ],
        axis=1,
    )

    def xy_copy(o):
        dx, dy = plane[o]
        return pltpu.make_async_remote_copy(
            src_ref=gram.at[0], dst_ref=gram_xy.at[o],
            send_sem=g_send.at[o], recv_sem=g_recv.at[o],
            device_id=device(dx=dx, dy=dy), device_id_type=MESH,
        )

    def zc_copy(o):
        dz, dc = column[o]
        return pltpu.make_async_remote_copy(
            src_ref=gram.at[1], dst_ref=gram_zc.at[o],
            send_sem=g_send.at[15 + o], recv_sem=g_recv.at[15 + o],
            device_id=device(dz=dz, dc=dc), device_id_type=MESH,
        )

    for o in range(15):
        xy_copy(o).start()
    total = gram[0]
    for o in range(15):
        xy_copy(o).wait_recv()
        total = total + gram_xy[o]
    gram[1] = total
    for o in range(15):
        zc_copy(o).start()
    for o in range(15):
        zc_copy(o).wait_recv()
        total = total + gram_zc[o]

    curvature, pr, pp = total[:, 0:16], total[:, 16:32], total[:, 32:48]
    rr, rp = total[:, 48:64], total[:, 64:80]
    curvature_inv, rr_inv = inverse(curvature), inverse(rr)
    alpha_t = nn(rr, curvature_inv)
    alpha = nn(curvature_inv, rr)
    residual_next = rest - nn(alpha_t, product)
    res_out[...] = residual_next
    sol_out[...] = sol_ref[...] + nn(alpha_t, way)
    new_gram = rr - nn(alpha_t, pr) + nn(nn(alpha_t, pp) - rp, alpha)
    beta_t = nn(new_gram, rr_inv)
    dir_out[...] = residual_next + nn(beta_t, way)

    for index in others:
        a_copy(index).wait_send()
        pa_copy(index).wait_send()
    for index in range(1, 9):
        z_copy(index).wait_send()
    for slot in range(8):
        c_copy(slot).wait_send()
    for slot in range(1, 16):
        b_copy(slot).wait_send()
    for o in range(15):
        xy_copy(o).wait_send()
        zc_copy(o).wait_send()


def shards(embeddings, solution, residual, direction):
    small = jax.ShapeDtypeStruct((rubrics, points), f32)
    vmem = pl.BlockSpec(memory_space=pltpu.VMEM)
    dma = pltpu.SemaphoreType.DMA
    return pl.pallas_call(
        kernel,
        out_shape=(small, small, small),
        in_specs=[vmem] * 4,
        out_specs=(vmem,) * 3,
        scratch_shapes=[
            pltpu.VMEM((16, deep, points), bf16),
            pltpu.VMEM((10, rows_sent, points), bf16),
            pltpu.VMEM((10 * points, deep), bf16),
            pltpu.VMEM((10 * points, 64), f32),
            pltpu.VMEM((16, 64, points), f32),
            pltpu.VMEM((512, 512), f32),
            pltpu.VMEM((512, 512), f32),
            pltpu.VMEM((10, rubrics, points), f32),
            pltpu.VMEM((16, rubrics, points), f32),
            pltpu.VMEM((10, rubrics, points), f32),
            pltpu.VMEM((16, rubrics, points), f32),
            pltpu.VMEM((2, rubrics, 128), f32),
            pltpu.VMEM((15, rubrics, 128), f32),
            pltpu.VMEM((15, rubrics, 128), f32),
            dma((10,)), dma((10,)), dma((9,)), dma((9,)), dma((8,)), dma((8,)),
            dma((10,)), dma((10,)), dma((16,)), dma((16,)), dma((30,)), dma((30,)),
        ],
        compiler_params=pltpu.CompilerParams(
            collective_id=0, has_side_effects=True, vmem_limit_bytes=48 * 2**20
        ),
        cost_estimate=pl.CostEstimate(
            flops=20_000_000_000, bytes_accessed=1_000_000, transcendentals=9_000_000
        ),
        name="iteration",
    )(embeddings, solution, residual, direction)


def solution(mesh):
    spec = P(None, ("row", "col"))
    return jax.shard_map(
        shards, mesh=mesh, in_specs=(spec,) * 4, out_specs=(spec,) * 3, check_vma=False
    )
```

time: 543 us -> 84.1 us (0.15)
  waiting for transfers between devices: 182 us -> 0 us
  blocking collectives: 172 us -> 0 us
  matrix products: 143 us -> 0 us
  Pallas kernels: 0 us -> 78.2 us
  other arithmetic: 13.2 us -> 0 us
  between operations: 13.8 us -> 0.65 us
  local copies, waits for them, and re-layouts: 14.6 us -> 4.89 us
    psum x2 -> x0, blocking collectives: 149 us -> none  [the longest x1 75.8 us: shards(): curvature, old_gram = lax.psum((local_curv, local_old), ('row', 'col'))]
    dot_general x134 -> x0, matrix products: 142 us -> none  [the longest x64 98.4 us: kernel_block(): cross = jnp.dot(col_piece.T, row_piece, preferred_element_type=jnp.float32)]
    all_gather x2 -> x0, waiting for transfers between devices: 98.8 us -> none  [the longest x1 71.1 us: shards(): row_points = lax.all_gather(embeddings, 'col', axis=1, tiled=True)]
    reduce_scatter x1 -> x0, waiting for transfers between devices: 82.3 us -> none  [shards(): lax.psum_scatter(applied, 'col', scatter_dimension=1, tiled=True)]
    pallas_call x0 -> x1, Pallas kernels: none -> 78.2 us  [shards(): pl.pallas_call(kernel, out_shape=(small, small, small), in_specs=[vmem] *...]
    all_gather x1 -> x0, blocking collectives: 22.4 us -> none  [shards(): col_weights = lax.all_gather(direction, 'row', axis=1, tiled=True)]
    dynamic_slice x80 -> x0, local copies, waits for them, and re-layouts: 13.6 us -> none  [the longest x8 8.22 us: row_step(): lax.dynamic_slice_in_dim(row_points, index_row * row_span, row_span, 1)]
    another operation x10 -> x0, other arithmetic: 8.01 us -> none  [the longest x6 4.26 us: spd_solve(): factor = jnp.linalg.cholesky(matrix)]
  transfers between devices with their start and end apart: 3 -> 0, of which waited for: 3 -> 0; matrix products, arithmetic and copies ran while one was open for 1% -> 0% of each run, Pallas kernels for 0% -> 0%
where the time goes in v1:
time: 84.1 us; the launch traced here: 83.7 us
  Pallas kernels  78.2 us (93%)
  local copies, waits for them, and re-layouts  4.89 us (6%)
    pallas_call x1, Pallas kernels, shards(): pl.pallas_call(kernel, out_shape=(small, small, small), in_specs=[vmem] *...  78.2 us
    unnamed x11, local copies, waits for them, and re-layouts  4.89 us

profile of v1, /device:TPU:1, one launch (start us, length us, event | category | flops | bytes accessed | tf_op | source)
XLA Modules:
  0.0 83.7 jit_solution(17465454139578063228)
XLA Ops:
  0.6 0.0 copy-start
  0.6 0.9 %copy-done = bf16[384,256]{1,0:T(8,128)(2,1)S(1)} copy-done((bf16[384,256]{1,0:T(8,128)(2,1)S(1)}, bf16[384,256]{1,0:T(8,128)(2,1)}, u32[]{:S(2)}) %copy-start) | copy-done | bytes 196632
  1.6 0.0 copy-start.1
  1.6 0.7 copy-done.1
  2.3 0.0 copy-start.2
  2.3 0.7 copy-done.2
  3.0 0.0 copy-start.3
  3.0 0.7 copy-done.3
  3.7 78.2 %iteration.1 = (f32[16,256]{1,0:T(8,128)S(1)}, f32[16,256]{1,0:T(8,128)S(1)}, f32[16,256]{1,0:T(8,128)S(1)}) custom-call(bf16[384,256]{1,0:T(8,128)(2,1)S(1)} %copy-done, f32[16,256]{1,0:T(8,128)S(1)} %copy-done.1, f32[16,256]{1,0:T(8,128)S(1)} %copy-done.2, f32[16,256]{1,0:T(8,128)S(1)} %copy-done.3), custom_call_target="tpu_custom_call" | custom-call | flops 20000000000 | bytes 1000000 | tf_op jit(solution)/shard_map/iteration/pallas_call | solution.py:420
  81.9 0.6 copy.10
  82.5 0.6 copy.11
  83.1 0.6 copy.12
Async XLA Ops:
  0.6 0.9 %copy-start = (bf16[384,256]{1,0:T(8,128)(2,1)S(1)}, bf16[384,256]{1,0:T(8,128)(2,1)}, u32[]{:S(2)}) copy-start(bf16[384,256]{1,0:T(8,128)(2,1)} %e_ref.1) | copy-start | bytes 589828
  1.6 0.7 copy-start.1
  2.3 0.7 copy-start.2
  3.0 0.7 copy-start.3

commit v2 on v1

v2 whole, which is shorter than its diff:
```python
import functools

import jax
import jax.numpy as jnp
from jax import lax
from jax.experimental import pallas as pl
from jax.experimental.pallas import tpu as pltpu
from jax.sharding import PartitionSpec as P

f32, bf16, f8 = jnp.float32, jnp.bfloat16, jnp.float8_e4m3fn
MESH = pl.DeviceIdType.MESH
highest = lax.Precision.HIGHEST

ridge_weight = 0.5
points = 256
rubrics = 16
width = 384
deep = 512
aug_at, hi_at, lo_at, rows_sent = 384, 400, 416, 432
low_scale, dir_scale, dir_step = 65536.0, 64.0, 16.0
scale = 4.0 / width

slots = [
    ((1, 0), (1, 0)),
    ((0, 3), (0, 3)),
    ((1, 3), (1, 0)),
    ((1, 1), (0, 1)),
    ((2, 1), (1, 0)),
    ((3, 2), (3, 0)),
    ((2, 0), (0, 3)),
    ((2, 2), (0, 1)),
    ((0, 0), None),
    ((0, 2), (0, 3)),
]
own = 8
others = [index for index in range(10) if index != own]
place = {offset: index for index, (offset, _) in enumerate(slots)}
along_z = [0, 1, 7, 2, 6, 3, 5, 4]
half_rows = 208
runs = [
    (3, 0, 0, 0, 1),
    (3, 1, 0, 0, 1),
    (2, 0, 0, 3, 1),
    (2, 1, 0, 3, 1),
    (1, 4, 0, 3, 0),
    (5, 2, 0, 0, 1),
    (3, 0, 1, 6, 0),
    (3, 0, 1, 5, 0),
    (5, 0, 1, 7, 0),
    (3, 3, 0, 5, -2),
    (1, 3, 0, 0, 0),
    (2, 4, 0, 5, -4),
    (1, 4, 0, 0, 0),
]
tiles = 34


def parent(index):
    (ox, oy), (hx, hy) = slots[index]
    return place[((ox - hx) % 4, (oy - hy) % 4)]


def tile_at(t):
    i, k, start = 0, 0, 0
    for count, i0, i_step, k0, k_step in runs:
        late = t - start
        i = jnp.where(late >= 0, i0 + late * i_step, i)
        k = jnp.where(late >= 0, k0 + late * k_step, k)
        start += count
    beyond = t >= start
    return jnp.where(beyond, 0, i), jnp.where(beyond, 0, k)


def nt(left, right, precision=None):
    return lax.dot_general(
        left, right, (((1,), (1,)), ((), ())), precision=precision, preferred_element_type=f32
    )


def nn(left, right):
    return jnp.dot(left, right, precision=highest, preferred_element_type=f32)


def low_parts(pieces):
    whole = pieces.astype(f32)
    whole = (whole[:rubrics] + whole[rubrics:]) * dir_scale
    first = whole.astype(f8)
    second = ((whole - first.astype(f32)) * dir_step).astype(f8)
    return jnp.concatenate([first, second], axis=0)


def combine(parts):
    low = parts[32:48] + parts[48:64] * (1.0 / dir_step)
    return parts[0:16] + parts[16:32] + low * (1.0 / (low_scale * dir_scale))


def pack(matrix):
    return jnp.concatenate([matrix[0:8], matrix[8:16]], axis=1)


def unpack(packed, at):
    return jnp.concatenate([packed[:, at : at + 16], packed[:, at + 16 : at + 32]], axis=0)


def inverse(matrix):
    size = matrix.shape[0]
    row = lax.broadcasted_iota(jnp.int32, matrix.shape, 0)
    col = lax.broadcasted_iota(jnp.int32, matrix.shape, 1)
    for step in range(size):
        pivot_row = matrix[step : step + 1, :]
        pivot_col = matrix[:, step : step + 1]
        pivot = 1.0 / matrix[step : step + 1, step : step + 1]
        scaled = pivot_row * pivot
        inner = matrix - pivot_col * scaled
        at_row, at_col = row == step, col == step
        matrix = jnp.where(
            at_row,
            jnp.where(at_col, pivot, scaled),
            jnp.where(at_col, -pivot_col * pivot, inner),
        )
    return matrix


def kernel(
    e_hbm, sol_hbm, res_hbm, dir_hbm, sol_out, res_out, dir_out,
    e_ref, sol_ref, res_ref, dir_ref,
    xb, xa, la, acc_a, acc_b, s0, s1, part_a, part_b, sum_a, sum_b, gram, gram_in, old, old_in,
    in_sem, a_send, a_recv, z_send, z_recv, c_send, c_recv, pa_send, pa_recv, pb_send, pb_recv,
    g_send, g_recv, o_send, o_recv,
):
    row, col = lax.axis_index("row"), lax.axis_index("col")
    core, x, z_lo = lax.rem(row, 2), lax.rem(lax.div(row, 2), 4), lax.div(row, 8)
    y, z_hi = lax.div(col, 4), lax.rem(col, 4)
    z = z_hi * 2 + z_lo

    def device(dx=0, dy=0, dz=0, dc=0):
        x2, y2 = lax.rem(x + dx % 4, 4), lax.rem(y + dy % 4, 4)
        z2, c2 = lax.rem(z + dz % 8, 8), lax.rem(core + dc, 2)
        return (lax.rem(z2, 2) * 8 + x2 * 2 + c2, y2 * 4 + lax.div(z2, 2))

    fetch = [
        pltpu.make_async_copy(source, into, in_sem.at[n])
        for n, (source, into) in enumerate(
            ((e_hbm, e_ref), (dir_hbm, dir_ref), (res_hbm, res_ref), (sol_hbm, sol_ref))
        )
    ]
    for copy in fetch:
        copy.start()
    barrier = pltpu.get_barrier_semaphore()
    neighbours = [
        device(dx=1), device(dx=3), device(dy=1), device(dy=3), device(dz=1), device(dz=7), device(dc=1)
    ]
    for neighbour in neighbours:
        pl.semaphore_signal(barrier, inc=1, device_id=neighbour, device_id_type=MESH)

    fetch[0].wait()
    fetch[1].wait()
    block = e_ref[...]
    wide = block.astype(f32)
    half = -0.5 * jnp.sum(wide * wide, axis=0, keepdims=True)
    h1 = half.astype(bf16).astype(f32)
    h2 = (half - h1).astype(bf16).astype(f32)
    h3 = half - h1 - h2
    at = lax.broadcasted_iota(jnp.int32, (16, points), 0)
    ones = jnp.where((at >= 8) & (at < 11), 1.0, 0.0)
    aug = jnp.where(at == 0, h1, jnp.where(at == 1, h2, jnp.where(at == 2, h3, ones)))
    way = dir_ref[...]
    way_hi = way.astype(bf16)
    way_lo = (way - way_hi.astype(f32)).astype(bf16)
    for buffer, slot in ((xb, 0), (xa, own)):
        buffer[slot, 0:width, :] = block
        buffer[slot, aug_at:hi_at, :] = aug.astype(bf16)
        buffer[slot, hi_at:lo_at, :] = way_hi
        buffer[slot, lo_at:rows_sent, :] = way_lo

    pl.semaphore_wait(barrier, len(neighbours))

    body_rows = pl.ds(0, rows_sent)

    def remote(source, target, send, recv, to):
        return pltpu.make_async_remote_copy(
            src_ref=source, dst_ref=target, send_sem=send, recv_sem=recv,
            device_id=to, device_id_type=MESH,
        )

    def a_copy(index):
        hx, hy = slots[index][1]
        return remote(
            xa.at[parent(index)], xa.at[index], a_send.at[index], a_recv.at[index], device(dx=-hx, dy=-hy)
        )

    def z_copy(index):
        slot = min(index, 7)
        source = [None, 0, 0, 1, 2, 3, 4, 5, 6][index]
        rows = body_rows
        if index == 7:
            rows = pl.ds(0, half_rows)
        if index == 8:
            rows = pl.ds(half_rows, rows_sent - half_rows)
        step = -1 if index in (1, 3, 5, 7) else 1
        return remote(
            xb.at[2 * source, rows, :], xb.at[2 * slot, rows, :], z_send.at[index], z_recv.at[index],
            device(dz=step),
        )

    def c_copy(slot):
        return remote(
            xb.at[2 * slot, body_rows, :], xb.at[2 * slot + 1, body_rows, :], c_send.at[slot], c_recv.at[slot],
            device(dc=1),
        )

    def turn(index):
        rows = pl.ds(index * points, points)
        la[rows, 0:width] = xa[index, 0:width, :].T
        extra = xa[index, aug_at:hi_at, :].astype(f32)
        extra = jnp.concatenate([extra[8:16], extra[0:8], jnp.zeros((112, points), f32)], axis=0)
        la[rows, width:deep] = extra.T.astype(bf16)

    for index in (0, 1):
        a_copy(index).start()
    for index in (1, 2):
        z_copy(index).start()
    c_copy(0).start()

    turn(own)
    xb[:, rows_sent:deep, :] = jnp.zeros((16, deep - rows_sent, points), bf16)
    acc_a[...] = jnp.zeros_like(acc_a)
    acc_b[...] = jnp.zeros_like(acc_b)
    fetch[2].wait()
    fetch[3].wait()
    rest = res_ref[...]
    empty = jnp.zeros((8, 96), f32)
    old[0] = jnp.concatenate([pack(nt(rest, rest, highest)), empty], axis=1)

    def cross(t, into):
        i, k = tile_at(t)
        left = la[pl.ds(pl.multiple_of(i * 512, 512), 512), :]
        into[:, 0:256] = jnp.dot(left, xb[2 * k], preferred_element_type=f32)
        into[:, 256:512] = jnp.dot(left, xb[2 * k + 1], preferred_element_type=f32)

    def consume(t, held):
        i, k = tile_at(t)
        weight = jnp.where((i >= 3) & ((k == 0) | (k == 7)), 0.5, 1.0).astype(f32)
        rows = pl.ds(pl.multiple_of(i * 512, 512), 512)
        values = jnp.exp(held[...] * scale)
        high = values.astype(bf16)
        low = ((values - high.astype(f32)) * low_scale).astype(f8)
        right = jnp.concatenate(
            [xb[2 * k, hi_at:rows_sent, :], xb[2 * k + 1, hi_at:rows_sent, :]], axis=1
        )
        acc_a[rows, 0:32] += nt(high, right) * weight
        acc_a[rows, 32:64] += nt(low, low_parts(right)) * weight
        left = jnp.concatenate(
            [xa[2 * i, hi_at:rows_sent, :], xa[2 * i + 1, hi_at:rows_sent, :]], axis=1
        )
        by_high = jnp.dot(left, high, preferred_element_type=f32) * weight
        by_low = jnp.dot(low_parts(left), low, preferred_element_type=f32) * weight
        for side in (0, 1):
            lanes = slice(side * 256, side * 256 + 256)
            acc_b[2 * k + side, 0:32, :] += by_high[:, lanes]
            acc_b[2 * k + side, 32:64, :] += by_low[:, lanes]

    def b_copy(slot):
        return remote(
            part_b.at[slot], sum_b.at[slot], pb_send.at[slot], pb_recv.at[slot],
            device(dz=along_z[slot // 2], dc=slot % 2),
        )

    def hand_b(*which):
        for k in which:
            for slot in (2 * k, 2 * k + 1):
                part_b[slot] = combine(acc_b[slot])
                if slot:
                    b_copy(slot).start()

    def pa_copy(index):
        ox, oy = slots[index][0]
        return remote(
            part_a.at[index], sum_a.at[index], pa_send.at[index], pa_recv.at[index], device(dx=ox, dy=oy)
        )

    def hand_a(*which):
        for index in which:
            part_a[index] = combine(acc_a[pl.ds(index * points, points), :].T)
            if index != own:
                pa_copy(index).start()

    def sum_copies(sent, landed, send, recv):
        copies = []
        for n in range(30):
            o = n % 15 + 1
            to = device(dx=o // 4, dy=o % 4) if n < 15 else device(dz=o // 2, dc=o % 2)
            copies.append(remote(sent.at[n // 15], landed.at[n], send.at[n], recv.at[n], to))
        return copies

    def start_stage(copies, stage):
        for copy in copies[15 * stage : 15 * stage + 15]:
            copy.start()

    def finish_stage(copies, sent, landed, stage):
        total = sent[stage]
        for n in range(15 * stage, 15 * stage + 15):
            copies[n].wait_recv()
            total = total + landed[n]
        return total

    old_copies = sum_copies(old, old_in, o_send, o_recv)
    gram_copies = sum_copies(gram, gram_in, g_send, g_recv)

    def first():
        for index in (0, 1):
            a_copy(index).wait_recv()
        for index in (1, 2):
            z_copy(index).wait_recv()
        for slot in (1, 2):
            c_copy(slot).start()
        for index in (9, 2, 3):
            a_copy(index).start()
        for index in (3, 4):
            z_copy(index).start()
        turn(0)
        turn(1)
        c_copy(0).wait_recv()

    def second():
        for index in (2, 3, 9):
            a_copy(index).wait_recv()
        for index in (3, 4):
            z_copy(index).wait_recv()
        for slot in (3, 4):
            c_copy(slot).start()
        for index in (4, 5):
            a_copy(index).start()
        for index in (5, 6):
            z_copy(index).start()
        for index in (2, 3, 9):
            turn(index)

    def third():
        for index in (4, 5):
            a_copy(index).wait_recv()
        for index in (5, 6):
            z_copy(index).wait_recv()
        for slot in (5, 6):
            c_copy(slot).start()
        for index in (6, 7):
            a_copy(index).start()
        for index in (7, 8):
            z_copy(index).start()
        for index in (4, 5):
            turn(index)

    def fourth():
        for index in (7, 8):
            z_copy(index).wait_recv()
        c_copy(7).start()
        for index in (6, 7):
            a_copy(index).wait_recv()
        for index in (6, 7):
            turn(index)

    def siblings(*which):
        for slot in which:
            c_copy(slot).wait_recv()

    def old_first():
        start_stage(old_copies, 0)

    def old_second():
        old[1] = finish_stage(old_copies, old, old_in, 0)
        start_stage(old_copies, 1)

    def old_third():
        old[2] = finish_stage(old_copies, old, old_in, 1)

    bind = functools.partial
    events = {
        0: [bind(siblings, 1, 2)],
        1: [second],
        2: [bind(siblings, 3, 4)],
        5: [third],
        7: [bind(siblings, 5, 6), bind(hand_b, 2)],
        8: [bind(hand_b, 4), old_first],
        9: [fourth],
        10: [bind(siblings, 7), bind(hand_b, 6)],
        11: [old_second],
        13: [bind(hand_a, 0, 1, 2, 3, 4, 5)],
        14: [bind(hand_b, 7), old_third],
        15: [bind(hand_b, 3)],
        16: [bind(hand_a, 6, 7), bind(hand_b, 5)],
    }

    first()
    cross(jnp.int32(0), s0)

    def step(n, carry):
        for at_step, acts in events.items():

            @pl.when(n == at_step)
            def _(acts=acts):
                for act in acts:
                    act()

        t = 2 * n
        cross(t + 1, s1)
        consume(t, s0)
        cross(t + 2, s0)
        consume(t + 1, s1)
        return carry

    lax.fori_loop(0, tiles // 2, step, 0)

    hand_a(9)
    hand_b(1, 0)
    hand_a(own)
    rr = unpack(old[2], 0)
    rr_inv = inverse(rr)
    product = part_a[own] + part_b[0] + ridge_weight * way
    for slot in (4, 5, 8, 9, 12, 13, 14, 15, 6, 7, 10, 11):
        b_copy(slot).wait_recv()
        product = product + sum_b[slot]
    for index in (0, 1, 2, 3, 4, 5, 6, 7, 9):
        pa_copy(index).wait_recv()
        product = product + sum_a[index]
    for slot in (1, 2, 3):
        b_copy(slot).wait_recv()
        product = product + sum_b[slot]

    by_product = nt(jnp.concatenate([way, product], axis=0), product, highest)
    of_product = nt(product, jnp.concatenate([way, rest], axis=0), highest)
    curvature = 0.5 * (by_product[0:16] + of_product[:, 0:16])
    gram[0] = jnp.concatenate(
        [pack(curvature), pack(of_product[:, 16:32]), pack(by_product[16:32]), empty[:, 0:32]], axis=1
    )
    start_stage(gram_copies, 0)
    gram[1] = finish_stage(gram_copies, gram, gram_in, 0)
    start_stage(gram_copies, 1)
    total = finish_stage(gram_copies, gram, gram_in, 1)

    curvature, pr, pp = unpack(total, 0), unpack(total, 32), unpack(total, 64)
    curvature_inv = inverse(curvature)
    alpha_t = nn(rr, curvature_inv)
    alpha = nn(curvature_inv, rr)
    residual_next = rest - nn(alpha_t, product)
    res_out[...] = residual_next
    sol_out[...] = sol_ref[...] + nn(alpha_t, way)
    crossed = nn(alpha_t, pr)
    new_gram = rr - crossed - crossed.T + nn(nn(alpha_t, pp), alpha)
    beta_t = nn(new_gram, rr_inv)
    dir_out[...] = residual_next + nn(beta_t, way)

    for index in others:
        a_copy(index).wait_send()
        pa_copy(index).wait_send()
    for index in range(1, 9):
        z_copy(index).wait_send()
    for slot in range(8):
        c_copy(slot).wait_send()
    for slot in range(1, 16):
        b_copy(slot).wait_send()
    for copy in old_copies + gram_copies:
        copy.wait_send()


def shards(embeddings, solution, residual, direction):
    small = jax.ShapeDtypeStruct((rubrics, points), f32)
    vmem = pl.BlockSpec(memory_space=pltpu.VMEM)
    dma = pltpu.SemaphoreType.DMA
    return pl.pallas_call(
        kernel,
        out_shape=(small, small, small),
        in_specs=[pl.BlockSpec(memory_space=pl.ANY)] * 4,
        out_specs=(vmem,) * 3,
        scratch_shapes=[
            pltpu.VMEM((width, points), bf16),
            pltpu.VMEM((rubrics, points), f32),
            pltpu.VMEM((rubrics, points), f32),
            pltpu.VMEM((rubrics, points), f32),
            pltpu.VMEM((16, deep, points), bf16),
            pltpu.VMEM((10, rows_sent, points), bf16),
            pltpu.VMEM((10 * points, deep), bf16),
            pltpu.VMEM((10 * points, 64), f32),
            pltpu.VMEM((16, 64, points), f32),
            pltpu.VMEM((512, 512), f32),
            pltpu.VMEM((512, 512), f32),
            pltpu.VMEM((10, rubrics, points), f32),
            pltpu.VMEM((16, rubrics, points), f32),
            pltpu.VMEM((10, rubrics, points), f32),
            pltpu.VMEM((16, rubrics, points), f32),
            pltpu.VMEM((2, 8, 128), f32),
            pltpu.VMEM((30, 8, 128), f32),
            pltpu.VMEM((3, 8, 128), f32),
            pltpu.VMEM((30, 8, 128), f32),
            dma((4,)), dma((10,)), dma((10,)), dma((9,)), dma((9,)), dma((8,)), dma((8,)),
            dma((10,)), dma((10,)), dma((16,)), dma((16,)), dma((30,)), dma((30,)), dma((30,)), dma((30,)),
        ],
        compiler_params=pltpu.CompilerParams(
            collective_id=0, has_side_effects=True, vmem_limit_bytes=56 * 2**20
        ),
        cost_estimate=pl.CostEstimate(
            flops=20_000_000_000, bytes_accessed=1_000_000, transcendentals=9_000_000
        ),
        name="iteration",
    )(embeddings, solution, residual, direction)


def solution(mesh):
    spec = P(None, ("row", "col"))
    return jax.shard_map(
        shards, mesh=mesh, in_specs=(spec,) * 4, out_specs=(spec,) * 3, check_vma=False
    )
```

time: 84.1 us -> 74.8 us (0.89)
  Pallas kernels: 78.2 us -> 71.2 us
  local copies, waits for them, and re-layouts: 4.89 us -> 2.66 us
    pallas_call x1, Pallas kernels: 78.2 us -> 71.2 us  [shards(): pl.pallas_call(kernel, out_shape=(small, small, small), in_specs=[pl.Bloc...]
    unnamed x11 -> x7, local copies, waits for them, and re-layouts: 4.89 us -> 2.66 us
where the time goes in v2:
time: 74.8 us; the launch traced here: 74.5 us
  Pallas kernels  71.2 us (95%)
  local copies, waits for them, and re-layouts  2.66 us (4%)
    pallas_call x1, Pallas kernels, shards(): pl.pallas_call(kernel, out_shape=(small, small, small), in_specs=[pl.Bloc...  71.2 us
    unnamed x7, local copies, waits for them, and re-layouts  2.66 us

profile of v2, /device:TPU:1, one launch (start us, length us, event | category | flops | bytes accessed | tf_op | source)
XLA Modules:
  0.0 74.5 jit_solution(11109598484080010803)
XLA Ops:
  0.6 71.2 %iteration.1 = (f32[16,256]{1,0:T(8,128)}, f32[16,256]{1,0:T(8,128)}, f32[16,256]{1,0:T(8,128)}) custom-call(bf16[384,256]{1,0:T(8,128)(2,1)} %e_hbm.1, f32[16,256]{1,0:T(8,128)} %sol_hbm.1, f32[16,256]{1,0:T(8,128)} %res_hbm.1, f32[16,256]{1,0:T(8,128)} %dir_hbm.1), custom_call_target="tpu_custom_call" | custom-call | flops 20000000000 | bytes 1000000 | tf_op jit(solution)/shard_map/iteration/pallas_call | solution.py:469
  71.9 0.0 copy-start.1
  71.9 1.3 %copy.10 = f32[16,256]{1,0:T(8,128)} copy(f32[16,256]{1,0:T(8,128)} %get-tuple-element.6) | data formatting | bytes 32768
  73.2 0.0 copy-done.1
  73.2 0.0 copy-start
  73.2 0.6 copy.11
  73.8 0.1 copy-done
  73.9 0.6 copy.12
Async XLA Ops:
  71.9 1.3 %copy-start.1 = (f32[16,256]{1,0:T(8,128)S(1)}, f32[16,256]{1,0:T(8,128)}, u32[]{:S(2)}) copy-start(f32[16,256]{1,0:T(8,128)} %get-tuple-element.7) | copy-start | bytes 49156
  73.2 0.7 copy-start

commit v3 on v2

--- a/solution.py
+++ b/solution.py
@@ -37,22 +37,17 @@
 place = {offset: index for index, (offset, _) in enumerate(slots)}
 along_z = [0, 1, 7, 2, 6, 3, 5, 4]
 half_rows = 208
-runs = [
-    (3, 0, 0, 0, 1),
-    (3, 1, 0, 0, 1),
-    (2, 0, 0, 3, 1),
-    (2, 1, 0, 3, 1),
-    (1, 4, 0, 3, 0),
-    (5, 2, 0, 0, 1),
-    (3, 0, 1, 6, 0),
-    (3, 0, 1, 5, 0),
-    (5, 0, 1, 7, 0),
-    (3, 3, 0, 5, -2),
-    (1, 3, 0, 0, 0),
-    (2, 4, 0, 5, -4),
-    (1, 4, 0, 0, 0),
+opening = [(0, 0), (0, 1), (0, 2)]
+main = [
+    [(1, 0), (1, 1), (1, 2), (4, 1)],
+    [(0, 3), (0, 4), (1, 3), (1, 4)],
+    [(2, 0), (2, 1), (2, 2), (2, 3)],
+    [(2, 4), (0, 6), (1, 6), (2, 6)],
+    [(0, 5), (1, 5), (2, 5), (4, 5)],
+    [(3, 5), (3, 3), (3, 1), (3, "both")],
+    [(0, 7), (1, 7), (2, 7), (4, 7)],
 ]
-tiles = 34
+closing = [(4, 3), (4, 0)]
 
 
 def parent(index):
@@ -60,15 +55,12 @@
     return place[((ox - hx) % 4, (oy - hy) % 4)]
 
 
-def tile_at(t):
-    i, k, start = 0, 0, 0
-    for count, i0, i_step, k0, k_step in runs:
-        late = t - start
-        i = jnp.where(late >= 0, i0 + late * i_step, i)
-        k = jnp.where(late >= 0, k0 + late * k_step, k)
-        start += count
-    beyond = t >= start
-    return jnp.where(beyond, 0, i), jnp.where(beyond, 0, k)
+def pick(n, values):
+    value = values[0]
+    for index in range(1, len(values)):
+        if values[index] != values[index - 1]:
+            value = jnp.where(n >= index, values[index], value)
+    return value
 
 
 def nt(left, right, precision=None):
@@ -103,28 +95,28 @@
 
 
 def inverse(matrix):
-    size = matrix.shape[0]
     row = lax.broadcasted_iota(jnp.int32, matrix.shape, 0)
     col = lax.broadcasted_iota(jnp.int32, matrix.shape, 1)
-    for step in range(size):
-        pivot_row = matrix[step : step + 1, :]
-        pivot_col = matrix[:, step : step + 1]
-        pivot = 1.0 / matrix[step : step + 1, step : step + 1]
-        scaled = pivot_row * pivot
-        inner = matrix - pivot_col * scaled
-        at_row, at_col = row == step, col == step
-        matrix = jnp.where(
-            at_row,
-            jnp.where(at_col, pivot, scaled),
-            jnp.where(at_col, -pivot_col * pivot, inner),
-        )
+    for s in range(0, matrix.shape[0], 2):
+        e = s + 1
+        one, two = matrix[s:e, :], matrix[e : e + 1, :]
+        col_one, col_two = matrix[:, s:e], matrix[:, e : e + 1]
+        a, b, c, d = one[:, s:e], one[:, e : e + 1], two[:, s:e], two[:, e : e + 1]
+        share = 1.0 / (a * d - b * c)
+        first, second = col == s, col == e
+        one = jnp.where(first[0:1], 1.0, jnp.where(second[0:1], 0.0, one))
+        two = jnp.where(first[0:1], 0.0, jnp.where(second[0:1], 1.0, two))
+        new_one = (d * share) * one - (b * share) * two
+        new_two = (a * share) * two - (c * share) * one
+        inner = jnp.where(first | second, 0.0, matrix) - col_one * new_one - col_two * new_two
+        matrix = jnp.where(row == s, new_one, jnp.where(row == e, new_two, inner))
     return matrix
 
 
 def kernel(
-    e_hbm, sol_hbm, res_hbm, dir_hbm, sol_out, res_out, dir_out,
+    e_hbm, sol_hbm, res_hbm, dir_hbm, out,
     e_ref, sol_ref, res_ref, dir_ref,
-    xb, xa, la, acc_a, acc_b, s0, s1, part_a, part_b, sum_a, sum_b, gram, gram_in, old, old_in,
+    xb, xa, la, acc_a, acc_b, part_a, part_b, sum_a, sum_b, gram, gram_in, old, old_in,
     in_sem, a_send, a_recv, z_send, z_recv, c_send, c_recv, pa_send, pa_recv, pb_send, pb_recv,
     g_send, g_recv, o_send, o_recv,
 ):
@@ -232,21 +224,15 @@
     empty = jnp.zeros((8, 96), f32)
     old[0] = jnp.concatenate([pack(nt(rest, rest, highest)), empty], axis=1)
 
-    def cross(t, into):
-        i, k = tile_at(t)
-        left = la[pl.ds(pl.multiple_of(i * 512, 512), 512), :]
-        into[:, 0:256] = jnp.dot(left, xb[2 * k], preferred_element_type=f32)
-        into[:, 256:512] = jnp.dot(left, xb[2 * k + 1], preferred_element_type=f32)
-
-    def consume(t, held):
-        i, k = tile_at(t)
-        weight = jnp.where((i >= 3) & ((k == 0) | (k == 7)), 0.5, 1.0).astype(f32)
+    def tile(i, one, two, weight):
         rows = pl.ds(pl.multiple_of(i * 512, 512), 512)
-        values = jnp.exp(held[...] * scale)
+        lhs = la[rows, :]
+        halves = [jnp.dot(lhs, xb[slot], preferred_element_type=f32) for slot in (one, two)]
+        values = jnp.exp(jnp.concatenate(halves, axis=1) * scale)
         high = values.astype(bf16)
         low = ((values - high.astype(f32)) * low_scale).astype(f8)
         right = jnp.concatenate(
-            [xb[2 * k, hi_at:rows_sent, :], xb[2 * k + 1, hi_at:rows_sent, :]], axis=1
+            [xb[one, hi_at:rows_sent, :], xb[two, hi_at:rows_sent, :]], axis=1
         )
         acc_a[rows, 0:32] += nt(high, right) * weight
         acc_a[rows, 32:64] += nt(low, low_parts(right)) * weight
@@ -255,10 +241,24 @@
         )
         by_high = jnp.dot(left, high, preferred_element_type=f32) * weight
         by_low = jnp.dot(low_parts(left), low, preferred_element_type=f32) * weight
-        for side in (0, 1):
-            lanes = slice(side * 256, side * 256 + 256)
-            acc_b[2 * k + side, 0:32, :] += by_high[:, lanes]
-            acc_b[2 * k + side, 32:64, :] += by_low[:, lanes]
+        for slot, lanes in ((one, slice(0, 256)), (two, slice(256, 512))):
+            acc_b[slot, 0:32, :] += by_high[:, lanes]
+            acc_b[slot, 32:64, :] += by_low[:, lanes]
+
+    mine = jnp.where(x < 2, 0, 1)
+
+    def run_tile(i, k):
+        tile(i, 2 * k, 2 * k + 1, 0.5 if i == 4 and k in (0, 7) else 1.0)
+
+    def run_tiles(n, groups):
+        i = pick(n, [i for i, _ in groups])
+        at_one = pick(n, [0 if k == "both" else 2 * k for _, k in groups])
+        at_two = pick(n, [14 if k == "both" else 2 * k + 1 for _, k in groups])
+        weight = pick(n, [0.5 if i == 4 and k in (0, 7) else 1.0 for i, k in groups])
+        if any(k == "both" for _, k in groups):
+            shift = pick(n, [1 if k == "both" else 0 for _, k in groups]) * mine
+            at_one, at_two = at_one + shift, at_two + shift
+        tile(i, at_one, at_two, weight)
 
     def b_copy(slot):
         return remote(
@@ -286,12 +286,13 @@
                 pa_copy(index).start()
 
     def sum_copies(sent, landed, send, recv):
-        copies = []
-        for n in range(30):
-            o = n % 15 + 1
-            to = device(dx=o // 4, dy=o % 4) if n < 15 else device(dz=o // 2, dc=o % 2)
-            copies.append(remote(sent.at[n // 15], landed.at[n], send.at[n], recv.at[n], to))
-        return copies
+        plane = sorted(range(1, 16), key=lambda o: -min(o // 4, 4 - o // 4) - min(o % 4, 4 - o % 4))
+        column = sorted(range(1, 16), key=lambda o: -min(o // 2, 8 - o // 2))
+        targets = [device(dx=o // 4, dy=o % 4) for o in plane]
+        targets += [device(dz=o // 2, dc=o % 2) for o in column]
+        return [
+            remote(sent.at[n // 15], landed.at[n], send.at[n], recv.at[n], to) for n, to in enumerate(targets)
+        ]
 
     def start_stage(copies, stage):
         for copy in copies[15 * stage : 15 * stage + 15]:
@@ -370,28 +371,26 @@
         old[1] = finish_stage(old_copies, old, old_in, 0)
         start_stage(old_copies, 1)
 
-    def old_third():
-        old[2] = finish_stage(old_copies, old, old_in, 1)
-
     bind = functools.partial
+    first()
+
+    def open_step(n, carry):
+        for slot in (1, 2):
+            pl.when(n == slot)(bind(siblings, slot))
+        run_tiles(n, opening)
+        return carry
+
+    lax.fori_loop(0, len(opening), open_step, 0)
+
     events = {
-        0: [bind(siblings, 1, 2)],
-        1: [second],
-        2: [bind(siblings, 3, 4)],
-        5: [third],
-        7: [bind(siblings, 5, 6), bind(hand_b, 2)],
-        8: [bind(hand_b, 4), old_first],
-        9: [fourth],
-        10: [bind(siblings, 7), bind(hand_b, 6)],
-        11: [old_second],
-        13: [bind(hand_a, 0, 1, 2, 3, 4, 5)],
-        14: [bind(hand_b, 7), old_third],
-        15: [bind(hand_b, 3)],
-        16: [bind(hand_a, 6, 7), bind(hand_b, 5)],
+        0: [second],
+        1: [bind(siblings, 3, 4)],
+        2: [third],
+        3: [bind(siblings, 5, 6), bind(hand_b, 2), old_first],
+        4: [fourth, bind(hand_b, 4, 6)],
+        5: [bind(siblings, 7), old_second],
+        6: [bind(hand_a, 6, 7), bind(hand_b, 5, 1)],
     }
-
-    first()
-    cross(jnp.int32(0), s0)
 
     def step(n, carry):
         for at_step, acts in events.items():
@@ -401,28 +400,30 @@
                 for act in acts:
                     act()
 
-        t = 2 * n
-        cross(t + 1, s1)
-        consume(t, s0)
-        cross(t + 2, s0)
-        consume(t + 1, s1)
+        for u in range(4):
+            run_tiles(n, [group[u] for group in main])
         return carry
 
-    lax.fori_loop(0, tiles // 2, step, 0)
-
+    lax.fori_loop(0, len(main), step, 0)
+
+    hand_b(7)
+    hand_a(4, 5, 2, 3, 0, 1)
+    run_tile(*closing[0])
+    hand_b(3)
+    run_tile(*closing[1])
     hand_a(9)
-    hand_b(1, 0)
+    hand_b(0)
     hand_a(own)
-    rr = unpack(old[2], 0)
+    rr = unpack(finish_stage(old_copies, old, old_in, 1), 0)
     rr_inv = inverse(rr)
     product = part_a[own] + part_b[0] + ridge_weight * way
-    for slot in (4, 5, 8, 9, 12, 13, 14, 15, 6, 7, 10, 11):
+    for slot in (4, 5, 8, 9, 12, 13, 10, 11, 2, 3, 14, 15):
         b_copy(slot).wait_recv()
         product = product + sum_b[slot]
     for index in (0, 1, 2, 3, 4, 5, 6, 7, 9):
         pa_copy(index).wait_recv()
         product = product + sum_a[index]
-    for slot in (1, 2, 3):
+    for slot in (6, 7, 1):
         b_copy(slot).wait_recv()
         product = product + sum_b[slot]
 
@@ -438,16 +439,15 @@
     total = finish_stage(gram_copies, gram, gram_in, 1)
 
     curvature, pr, pp = unpack(total, 0), unpack(total, 32), unpack(total, 64)
-    curvature_inv = inverse(curvature)
-    alpha_t = nn(rr, curvature_inv)
-    alpha = nn(curvature_inv, rr)
+    residual_part = nn(pr, rr_inv)
+    stacked = jnp.concatenate([rr, pp, pr.T], axis=0)
+    by_curvature = nn(stacked, inverse(curvature))
+    alpha_t, pp_part, rp_part = by_curvature[0:16], by_curvature[16:32], by_curvature[32:48]
+    changed = nn(alpha_t, pp_part - residual_part)
     residual_next = rest - nn(alpha_t, product)
-    res_out[...] = residual_next
-    sol_out[...] = sol_ref[...] + nn(alpha_t, way)
-    crossed = nn(alpha_t, pr)
-    new_gram = rr - crossed - crossed.T + nn(nn(alpha_t, pp), alpha)
-    beta_t = nn(new_gram, rr_inv)
-    dir_out[...] = residual_next + nn(beta_t, way)
+    out[16:32] = residual_next
+    out[0:16] = sol_ref[...] + nn(alpha_t, way)
+    out[32:48] = residual_next + way + nn(changed - rp_part, way)
 
     for index in others:
         a_copy(index).wait_send()
@@ -463,14 +463,13 @@
 
 
 def shards(embeddings, solution, residual, direction):
-    small = jax.ShapeDtypeStruct((rubrics, points), f32)
     vmem = pl.BlockSpec(memory_space=pltpu.VMEM)
     dma = pltpu.SemaphoreType.DMA
-    return pl.pallas_call(
+    stacked = pl.pallas_call(
         kernel,
-        out_shape=(small, small, small),
+        out_shape=jax.ShapeDtypeStruct((3 * rubrics, points), f32),
         in_specs=[pl.BlockSpec(memory_space=pl.ANY)] * 4,
-        out_specs=(vmem,) * 3,
+        out_specs=vmem,
         scratch_shapes=[
             pltpu.VMEM((width, points), bf16),
             pltpu.VMEM((rubrics, points), f32),
@@ -481,15 +480,13 @@
             pltpu.VMEM((10 * points, deep), bf16),
             pltpu.VMEM((10 * points, 64), f32),
             pltpu.VMEM((16, 64, points), f32),
-            pltpu.VMEM((512, 512), f32),
-            pltpu.VMEM((512, 512), f32),
             pltpu.VMEM((10, rubrics, points), f32),
             pltpu.VMEM((16, rubrics, points), f32),
             pltpu.VMEM((10, rubrics, points), f32),
             pltpu.VMEM((16, rubrics, points), f32),
             pltpu.VMEM((2, 8, 128), f32),
             pltpu.VMEM((30, 8, 128), f32),
-            pltpu.VMEM((3, 8, 128), f32),
+            pltpu.VMEM((2, 8, 128), f32),
             pltpu.VMEM((30, 8, 128), f32),
             dma((4,)), dma((10,)), dma((10,)), dma((9,)), dma((9,)), dma((8,)), dma((8,)),
             dma((10,)), dma((10,)), dma((16,)), dma((16,)), dma((30,)), dma((30,)), dma((30,)), dma((30,)),
@@ -502,6 +499,7 @@
         ),
         name="iteration",
     )(embeddings, solution, residual, direction)
+    return stacked[0:16], stacked[16:32], stacked[32:48]
 
 
 def solution(mesh):

time: 74.8 us -> 66.9 us (0.89)
  Pallas kernels: 71.2 us -> 64.7 us
  local copies, waits for them, and re-layouts: 2.66 us -> 1.37 us
    pallas_call x1, Pallas kernels: 71.2 us -> 64.7 us  [shards(): pl.pallas_call(kernel, out_shape=jax.ShapeDtypeStruct((3 * rubrics, point...]
    unnamed x7 -> x0, local copies, waits for them, and re-layouts: 2.66 us -> none
    slice x0 -> x1, local copies, waits for them, and re-layouts: none -> 1.37 us  [shards(): return (stacked[0:16], stacked[16:32], stacked[32:48])]
where the time goes in v3:
time: 66.9 us; the launch traced here: 66.8 us
  Pallas kernels  64.7 us (97%)
  local copies, waits for them, and re-layouts  1.37 us (2%)
    pallas_call x1, Pallas kernels, shards(): pl.pallas_call(kernel, out_shape=jax.ShapeDtypeStruct((3 * rubrics, point...  64.7 us
    slice x1, local copies, waits for them, and re-layouts, shards(): return (stacked[0:16], stacked[16:32], stacked[32:48])  1.37 us

profile of v3, /device:TPU:1, one launch (start us, length us, event | category | flops | bytes accessed | tf_op | source)
XLA Modules:
  0.0 66.8 jit_solution(11760502721683319808)
XLA Ops:
  0.6 64.7 %iteration.1 = f32[48,256]{1,0:T(8,128)} custom-call(bf16[384,256]{1,0:T(8,128)(2,1)} %e_hbm.1, f32[16,256]{1,0:T(8,128)} %sol_hbm.1, f32[16,256]{1,0:T(8,128)} %res_hbm.1, f32[16,256]{1,0:T(8,128)} %dir_hbm.1), custom_call_target="tpu_custom_call" | custom-call | flops 20000000000 | bytes 1000000 | tf_op jit(solution)/shard_map/iteration/pallas_call | solution.py:468
  65.4 1.4 %fusion = (f32[16,256]{1,0:T(8,128)}, f32[16,256]{1,0:T(8,128)}, f32[16,256]{1,0:T(8,128)}) fusion(f32[48,256]{1,0:T(8,128)} %iteration.1), kind=kLoop, calls=%fused_computation | loop fusion | bytes 98304 | tf_op jit(solution)/shard_map/slice | solution.py:502

commit v4 on v3

v4 whole, which is shorter than its diff:
```python
import jax
import jax.numpy as jnp
from jax import lax
from jax.experimental import pallas as pl
from jax.experimental.pallas import tpu as pltpu
from jax.sharding import PartitionSpec as P

f32, bf16, f8 = jnp.float32, jnp.bfloat16, jnp.float8_e4m3fn
MESH = pl.DeviceIdType.MESH
highest = lax.Precision.HIGHEST

ridge_weight = 0.5
points = 256
rubrics = 16
width = 384
deep = 512
aug_at, hi_at, lo_at, rows_sent = 384, 400, 416, 432
low_scale, dir_scale, dir_step = 65536.0, 64.0, 16.0
scale = 4.0 / width

slots = [
    ((1, 0), (1, 0)),
    ((0, 3), (0, 3)),
    ((3, 1), (3, 1)),
    ((3, 2), (3, 0)),
    ((1, 1), (0, 1)),
    ((2, 1), (3, 0)),
    ((2, 0), (1, 0)),
    ((0, 2), (0, 3)),
    ((2, 2), (0, 1)),
    ((0, 0), None),
]
own = 9
others = [index for index in range(10) if index != own]
place = {offset: index for index, (offset, _) in enumerate(slots)}
along_z = [0, 1, 7, 2, 6, 3, 5, 4]
halves = ((0, 208), (208, 224))


def parent(index):
    (ox, oy), (hx, hy) = slots[index]
    return place[((ox - hx) % 4, (oy - hy) % 4)]


def nt(left, right, precision=None):
    return lax.dot_general(
        left, right, (((1,), (1,)), ((), ())), precision=precision, preferred_element_type=f32
    )


def nn(left, right):
    return jnp.dot(left, right, precision=highest, preferred_element_type=f32)


def low_parts(pieces):
    whole = pieces.astype(f32)
    whole = (whole[:rubrics] + whole[rubrics:]) * dir_scale
    first = whole.astype(f8)
    second = ((whole - first.astype(f32)) * dir_step).astype(f8)
    return jnp.concatenate([first, second], axis=0)


def combine(parts):
    low = parts[32:48] + parts[48:64] * (1.0 / dir_step)
    return parts[0:16] + parts[16:32] + low * (1.0 / (low_scale * dir_scale))


def pack(matrix):
    return jnp.concatenate([matrix[0:8], matrix[8:16]], axis=1)


def unpack(packed, at):
    return jnp.concatenate([packed[:, at : at + 16], packed[:, at + 16 : at + 32]], axis=0)


def inverse(matrix):
    row = lax.broadcasted_iota(jnp.int32, matrix.shape, 0)
    col = lax.broadcasted_iota(jnp.int32, matrix.shape, 1)
    for s in range(0, matrix.shape[0], 2):
        e = s + 1
        one, two = matrix[s:e, :], matrix[e : e + 1, :]
        col_one, col_two = matrix[:, s:e], matrix[:, e : e + 1]
        a, b, c, d = one[:, s:e], one[:, e : e + 1], two[:, s:e], two[:, e : e + 1]
        share = 1.0 / (a * d - b * c)
        first, second = col == s, col == e
        one = jnp.where(first[0:1], 1.0, jnp.where(second[0:1], 0.0, one))
        two = jnp.where(first[0:1], 0.0, jnp.where(second[0:1], 1.0, two))
        new_one = (d * share) * one - (b * share) * two
        new_two = (a * share) * two - (c * share) * one
        inner = jnp.where(first | second, 0.0, matrix) - col_one * new_one - col_two * new_two
        matrix = jnp.where(row == s, new_one, jnp.where(row == e, new_two, inner))
    return matrix


def kernel(
    e_hbm, sol_hbm, res_hbm, dir_hbm, out,
    e_ref, sol_ref, res_ref, dir_ref,
    xb, xa, la, acc_a, acc_b, part_a, part_b, sum_a, sum_b, gram, gram_in, old, old_in, curv, curv_in,
    in_sem, a_send, a_recv, z_send, z_recv, c_send, c_recv, pa_send, pa_recv, pb_send, pb_recv,
    g_send, g_recv, o_send, o_recv, q_send, q_recv,
):
    row, col = lax.axis_index("row"), lax.axis_index("col")
    core, x, z_lo = lax.rem(row, 2), lax.rem(lax.div(row, 2), 4), lax.div(row, 8)
    y, z_hi = lax.div(col, 4), lax.rem(col, 4)
    z = z_hi * 2 + z_lo

    def device(dx=0, dy=0, dz=0, dc=0):
        x2, y2 = lax.rem(x + dx % 4, 4), lax.rem(y + dy % 4, 4)
        z2, c2 = lax.rem(z + dz % 8, 8), lax.rem(core + dc, 2)
        return (lax.rem(z2, 2) * 8 + x2 * 2 + c2, y2 * 4 + lax.div(z2, 2))

    barrier = pltpu.get_barrier_semaphore()
    neighbours = [
        device(dx=1), device(dx=3), device(dy=1), device(dy=3), device(dz=1), device(dz=7), device(dc=1),
        device(dx=3, dy=1),
    ]
    for neighbour in neighbours:
        pl.semaphore_signal(barrier, inc=1, device_id=neighbour, device_id_type=MESH)
    fetch = [
        pltpu.make_async_copy(source, into, in_sem.at[n])
        for n, (source, into) in enumerate(
            ((e_hbm, e_ref), (dir_hbm, dir_ref), (res_hbm, res_ref), (sol_hbm, sol_ref))
        )
    ]
    for copy in fetch:
        copy.start()

    fetch[0].wait()
    fetch[1].wait()
    block = e_ref[...]
    wide = block.astype(f32)
    half = -0.5 * jnp.sum(wide * wide, axis=0, keepdims=True)
    h1 = half.astype(bf16).astype(f32)
    h2 = (half - h1).astype(bf16).astype(f32)
    h3 = half - h1 - h2
    at = lax.broadcasted_iota(jnp.int32, (16, points), 0)
    ones = jnp.where((at >= 8) & (at < 11), 1.0, 0.0)
    aug = jnp.where(at == 0, h1, jnp.where(at == 1, h2, jnp.where(at == 2, h3, ones)))
    way = dir_ref[...]
    way_hi = way.astype(bf16)
    way_lo = (way - way_hi.astype(f32)).astype(bf16)
    for buffer, slot in ((xb, 0), (xa, own)):
        buffer[slot, 0:width, :] = block
        buffer[slot, aug_at:hi_at, :] = aug.astype(bf16)
        buffer[slot, hi_at:lo_at, :] = way_hi
        buffer[slot, lo_at:rows_sent, :] = way_lo

    pl.semaphore_wait(barrier, len(neighbours))

    body_rows = pl.ds(0, rows_sent)

    def remote(source, target, send, recv, to):
        return pltpu.make_async_remote_copy(
            src_ref=source, dst_ref=target, send_sem=send, recv_sem=recv,
            device_id=to, device_id_type=MESH,
        )

    def a_copy(index, part):
        hx, hy = slots[index][1]
        rows = pl.ds(*halves[part])
        return remote(
            xa.at[parent(index), rows, :], xa.at[index, rows, :],
            a_send.at[index, part], a_recv.at[index, part], device(dx=-hx, dy=-hy),
        )

    def z_copy(index, part):
        source = [None, 0, 0, 1, 2, 3, 4, 5, 6][index]
        rows = pl.ds(*halves[part])
        step = -1 if index in (1, 3, 5, 7) else 1
        return remote(
            xb.at[2 * source, rows, :], xb.at[2 * min(index, 7), rows, :],
            z_send.at[index, part], z_recv.at[index, part], device(dz=step),
        )

    def z_part(index, n):
        return n if index % 2 else 1 - n

    def c_copy(slot):
        return remote(
            xb.at[2 * slot, body_rows, :], xb.at[2 * slot + 1, body_rows, :], c_send.at[slot], c_recv.at[slot],
            device(dc=1),
        )

    def turn(index):
        rows = pl.ds(index * points, points)
        la[rows, 0:width] = xa[index, 0:width, :].T
        extra = xa[index, aug_at:hi_at, :].astype(f32)
        extra = jnp.concatenate([extra[8:16], extra[0:8], jnp.zeros((112, points), f32)], axis=0)
        la[rows, width:deep] = extra.T.astype(bf16)

    for n in (0, 1):
        for index in (1, 2):
            z_copy(index, z_part(index, n)).start()
        for index in (0, 1, 2):
            a_copy(index, n).start()
    c_copy(0).start()

    turn(own)
    xb[:, rows_sent:deep, :] = jnp.zeros((16, deep - rows_sent, points), bf16)
    acc_a[...] = jnp.zeros_like(acc_a)
    acc_b[...] = jnp.zeros_like(acc_b)
    fetch[2].wait()
    fetch[3].wait()
    rest = res_ref[...]
    empty = jnp.zeros((8, 96), f32)
    old[0] = jnp.concatenate([pack(nt(rest, rest, highest)), empty], axis=1)

    def split(lhs, z_blocks):
        parts = [jnp.dot(lhs, xb[block], preferred_element_type=f32) for block in z_blocks]
        values = jnp.exp(jnp.concatenate(parts, axis=1) * scale)
        high = values.astype(bf16)
        return high, ((values - high.astype(f32)) * low_scale).astype(f8)

    def apply_rows(rows, right, right_low, high, low):
        acc_a[rows, 0:32] += nt(high, right)
        acc_a[rows, 32:64] += nt(low, right_low)

    def directions(z_blocks):
        right = jnp.concatenate([xb[block, hi_at:rows_sent, :] for block in z_blocks], axis=1)
        return right, low_parts(right)

    def both(*z_slots):
        return [block for k in z_slots for block in (2 * k, 2 * k + 1)]

    def tile(first_slots, z_blocks):
        runs = [(first * points, count * points) for first, count in first_slots]
        lhs = [la[pl.ds(*run), :] for run in runs]
        high, low = split(jnp.concatenate(lhs, axis=0) if len(lhs) > 1 else lhs[0], z_blocks)
        right, right_low = directions(z_blocks)
        start = 0
        for run in runs:
            part = slice(start, start + run[1])
            apply_rows(pl.ds(*run), right, right_low, high[part], low[part])
            start += run[1]
        left = [xa[first + n, hi_at:rows_sent, :] for first, count in first_slots for n in range(count)]
        left = jnp.concatenate(left, axis=1) if len(left) > 1 else left[0]
        by_high = jnp.dot(left, high, preferred_element_type=f32)
        by_low = jnp.dot(low_parts(left), low, preferred_element_type=f32)
        for n, block in enumerate(z_blocks):
            lanes = slice(n * points, (n + 1) * points)
            acc_b[block, 0:32, :] += by_high[:, lanes]
            acc_b[block, 32:64, :] += by_low[:, lanes]

    def own_tile(z_blocks):
        rows = pl.ds(own * points, points)
        apply_rows(rows, *directions(z_blocks), *split(la[rows, :], z_blocks))

    low_x, low_y = x < 2, y < 2
    mine = jnp.where(low_x, 0, 1)
    mine_other = jnp.where(low_x == low_y, 0, 1)

    def b_copy(slot):
        return remote(
            part_b.at[slot], sum_b.at[slot], pb_send.at[slot], pb_recv.at[slot],
            device(dz=along_z[slot // 2], dc=slot % 2),
        )

    def hand_b(*which):
        for k in which:
            for slot in (2 * k, 2 * k + 1):
                part_b[slot] = combine(acc_b[slot])
                if slot:
                    b_copy(slot).start()

    def pa_copy(index):
        ox, oy = slots[index][0]
        return remote(
            part_a.at[index], sum_a.at[index], pa_send.at[index], pa_recv.at[index], device(dx=ox, dy=oy)
        )

    def hand_a(*which):
        for index in which:
            part_a[index] = combine(acc_a[pl.ds(index * points, points), :].T)
            if index != own:
                pa_copy(index).start()

    def sum_copies(sent, landed, send, recv):
        plane = sorted(range(1, 16), key=lambda o: -min(o // 4, 4 - o // 4) - min(o % 4, 4 - o % 4))
        column = sorted(range(1, 16), key=lambda o: -min(o // 2, 8 - o // 2))
        targets = [device(dx=o // 4, dy=o % 4) for o in plane]
        targets += [device(dz=o // 2, dc=o % 2) for o in column]
        return [
            remote(sent.at[n // 15], landed.at[n], send.at[n], recv.at[n], to) for n, to in enumerate(targets)
        ]

    def start_stage(copies, stage):
        for copy in copies[15 * stage : 15 * stage + 15]:
            copy.start()

    def finish_stage(copies, sent, landed, stage):
        total = sent[stage]
        for n in range(15 * stage, 15 * stage + 15):
            copies[n].wait_recv()
            total = total + landed[n]
        return total

    old_copies = sum_copies(old, old_in, o_send, o_recv)
    gram_copies = sum_copies(gram, gram_in, g_send, g_recv)
    curv_copies = sum_copies(curv, curv_in, q_send, q_recv)

    def relay(n, z_in, z_out, a_in, a_out):
        for index in z_in:
            z_copy(index, z_part(index, n)).wait_recv()
        for index in z_out:
            z_copy(index, z_part(index, n)).start()
        if n == 1:
            for slot in z_in:
                c_copy(slot).start()
        for index in a_in:
            a_copy(index, n).wait_recv()
        for index in a_out:
            a_copy(index, n).start()

    def siblings(*which):
        for slot in which:
            c_copy(slot).wait_recv()

    def old_first():
        start_stage(old_copies, 0)

    def old_second():
        old[1] = finish_stage(old_copies, old, old_in, 0)
        start_stage(old_copies, 1)

    for n in (0, 1):
        relay(n, (1, 2), (3, 4), (0, 1, 2), (7, 4, 5, 6))
    for index in (0, 1, 2):
        turn(index)
    siblings(0)
    tile([(0, 3)], both(0))
    siblings(1, 2)
    own_tile(both(0, 1))
    relay(0, (3, 4), (5, 6), (7, 4, 5, 6), (3, 8))
    tile([(0, 3)], both(1, 2))
    relay(1, (3, 4), (5, 6), (7, 4, 5, 6), (3, 8))
    for index in (4, 5, 6, 7):
        turn(index)
    tile([(4, 2)], both(0, 1, 2))
    old_first()
    siblings(3, 4)
    relay(0, (5, 6), (7, 8), (3, 8), ())
    tile([(0, 2), (4, 2)], both(3, 4))
    own_tile(both(2))
    relay(1, (5, 6), (), (3, 8), ())
    for index in (3, 8):
        turn(index)
    tile([(3, 1)], both(0, 1, 2))
    hand_b(2)
    tile([(2, 2)], both(3, 4))
    hand_b(4)
    siblings(5, 6)
    tile([(0, 2), (4, 2)], both(5, 6))
    for index in (7, 8):
        z_copy(index, z_part(index, 0)).wait_recv()
    c_copy(7).start()
    old_second()
    tile([(8, 1)], both(1, 3))
    siblings(7)
    tile([(0, 6)], both(7))
    hand_a(4, 5, 0, 1)
    tile([(8, 1)], both(5) + [mine, 14 + mine])
    hand_a(8)
    tile([(6, 2)], both(5) + [mine_other, 14 + mine_other])
    hand_b(7, 0)
    tile([(2, 2)], both(5, 6))
    hand_a(3, 2)
    hand_b(5, 6)
    tile([(6, 2)], both(1, 3))
    hand_a(6, 7)
    hand_b(3, 1)
    own_tile(both(3, 4))
    own_tile(both(5, 6, 7))
    hand_a(own)

    ways = [
        xa[index, hi_at:lo_at, :].astype(f32) + xa[index, lo_at:rows_sent, :].astype(f32) for index in others
    ]
    partials = [part_a[index] for index in others]
    held = nt(jnp.concatenate(ways, axis=1), jnp.concatenate(partials, axis=1), highest)
    held = held + 0.5 * nt(way, part_a[own] + ridge_weight * way, highest)
    curv[0] = jnp.concatenate([pack(held + held.T), empty], axis=1)
    start_stage(curv_copies, 0)

    rr = unpack(finish_stage(old_copies, old, old_in, 1), 0)
    rr_inv = inverse(rr)
    product = part_a[own] + part_b[0] + ridge_weight * way
    for slot in (4, 5, 8, 9, 14, 15, 1, 10, 11, 12, 13):
        b_copy(slot).wait_recv()
        product = product + sum_b[slot]
    for index in (0, 1, 4, 5, 8, 2, 3, 6, 7):
        pa_copy(index).wait_recv()
        product = product + sum_a[index]
    for slot in (2, 3, 6, 7):
        b_copy(slot).wait_recv()
        product = product + sum_b[slot]

    with_rest = nt(product, jnp.concatenate([product, rest], axis=0), highest)
    gram[0] = jnp.concatenate([pack(with_rest[:, 16:32]), pack(with_rest[:, 0:16]), empty[:, 0:64]], axis=1)
    start_stage(gram_copies, 0)
    curv[1] = finish_stage(curv_copies, curv, curv_in, 0)
    start_stage(curv_copies, 1)
    gram[1] = finish_stage(gram_copies, gram, gram_in, 0)
    start_stage(gram_copies, 1)

    curvature_inv = inverse(unpack(finish_stage(curv_copies, curv, curv_in, 1), 0))
    alpha_t = nn(rr, curvature_inv)
    turned = nn(jnp.concatenate([curvature_inv, rr_inv], axis=0), way)
    residual_next = rest - nn(alpha_t, product)
    out[16:32] = residual_next
    out[0:16] = sol_ref[...] + nn(alpha_t, way)
    moved = residual_next + way

    total = finish_stage(gram_copies, gram, gram_in, 1)
    pr, pp = unpack(total, 0), unpack(total, 32)
    inner = nn(jnp.concatenate([pp, -pr], axis=1), turned)
    out[32:48] = moved + nn(alpha_t, inner) - nn(pr.T, turned[0:16])

    for index in others:
        pa_copy(index).wait_send()
        for part in (0, 1):
            a_copy(index, part).wait_send()
    for index in range(1, 9):
        for n in (0, 1) if index < 7 else (0,):
            z_copy(index, z_part(index, n)).wait_send()
    for slot in range(8):
        c_copy(slot).wait_send()
    for slot in range(1, 16):
        b_copy(slot).wait_send()
    for copy in old_copies + gram_copies + curv_copies:
        copy.wait_send()


def shards(embeddings, solution, residual, direction):
    vmem = pl.BlockSpec(memory_space=pltpu.VMEM)
    dma = pltpu.SemaphoreType.DMA
    stacked = pl.pallas_call(
        kernel,
        out_shape=jax.ShapeDtypeStruct((3 * rubrics, points), f32),
        in_specs=[pl.BlockSpec(memory_space=pl.ANY)] * 4,
        out_specs=vmem,
        scratch_shapes=[
            pltpu.VMEM((width, points), bf16),
            pltpu.VMEM((rubrics, points), f32),
            pltpu.VMEM((rubrics, points), f32),
            pltpu.VMEM((rubrics, points), f32),
            pltpu.VMEM((16, deep, points), bf16),
            pltpu.VMEM((10, rows_sent, points), bf16),
            pltpu.VMEM((10 * points, deep), bf16),
            pltpu.VMEM((10 * points, 64), f32),
            pltpu.VMEM((16, 64, points), f32),
            pltpu.VMEM((10, rubrics, points), f32),
            pltpu.VMEM((16, rubrics, points), f32),
            pltpu.VMEM((10, rubrics, points), f32),
            pltpu.VMEM((16, rubrics, points), f32),
            pltpu.VMEM((2, 8, 128), f32),
            pltpu.VMEM((30, 8, 128), f32),
            pltpu.VMEM((2, 8, 128), f32),
            pltpu.VMEM((30, 8, 128), f32),
            pltpu.VMEM((2, 8, 128), f32),
            pltpu.VMEM((30, 8, 128), f32),
            dma((4,)), dma((10, 2)), dma((10, 2)), dma((9, 2)), dma((9, 2)), dma((8,)), dma((8,)),
            dma((10,)), dma((10,)), dma((16,)), dma((16,)), dma((30,)), dma((30,)), dma((30,)), dma((30,)),
            dma((30,)), dma((30,)),
        ],
        compiler_params=pltpu.CompilerParams(
            collective_id=0, has_side_effects=True, vmem_limit_bytes=56 * 2**20
        ),
        cost_estimate=pl.CostEstimate(
            flops=20_000_000_000, bytes_accessed=1_000_000, transcendentals=9_000_000
        ),
        name="iteration",
    )(embeddings, solution, residual, direction)
    return stacked[0:16], stacked[16:32], stacked[32:48]


def solution(mesh):
    spec = P(None, ("row", "col"))
    return jax.shard_map(
        shards, mesh=mesh, in_specs=(spec,) * 4, out_specs=(spec,) * 3, check_vma=False
    )
```

time: 66.9 us -> 65.3 us (0.976)
  Pallas kernels: 64.7 us -> 63.1 us
    pallas_call x1, Pallas kernels: 64.7 us -> 63.1 us  [shards(): pl.pallas_call(kernel, out_shape=jax.ShapeDtypeStruct((3 * rubrics, point...]
where the time goes in v4:
time: 65.3 us; the launch traced here: 65.1 us
  Pallas kernels  63.1 us (97%)
  local copies, waits for them, and re-layouts  1.37 us (2%)
    pallas_call x1, Pallas kernels, shards(): pl.pallas_call(kernel, out_shape=jax.ShapeDtypeStruct((3 * rubrics, point...  63.1 us
    slice x1, local copies, waits for them, and re-layouts, shards(): return (stacked[0:16], stacked[16:32], stacked[32:48])  1.37 us

profile of v4, /device:TPU:1, one launch (start us, length us, event | category | flops | bytes accessed | tf_op | source)
XLA Modules:
  0.0 65.1 jit_solution(12071659638935410207)
XLA Ops:
  0.6 63.1 %iteration.1 = f32[48,256]{1,0:T(8,128)} custom-call(bf16[384,256]{1,0:T(8,128)(2,1)} %e_hbm.1, f32[16,256]{1,0:T(8,128)} %sol_hbm.1, f32[16,256]{1,0:T(8,128)} %res_hbm.1, f32[16,256]{1,0:T(8,128)} %dir_hbm.1), custom_call_target="tpu_custom_call" | custom-call | flops 20000000000 | bytes 1000000 | tf_op jit(solution)/shard_map/iteration/pallas_call | solution.py:436
  63.7 1.4 %fusion = (f32[16,256]{1,0:T(8,128)}, f32[16,256]{1,0:T(8,128)}, f32[16,256]{1,0:T(8,128)}) fusion(f32[48,256]{1,0:T(8,128)} %iteration.1), kind=kLoop, calls=%fused_computation | loop fusion | bytes 98304 | tf_op jit(solution)/shard_map/slice | solution.py:473

commit v5 on v4

--- a/solution.py
+++ b/solution.py
@@ -308,8 +308,9 @@
                 c_copy(slot).start()
         for index in a_in:
             a_copy(index, n).wait_recv()
-        for index in a_out:
-            a_copy(index, n).start()
+            for onward in a_out:
+                if parent(onward) == index:
+                    a_copy(onward, n).start()
 
     def siblings(*which):
         for slot in which:
@@ -328,35 +329,36 @@
         turn(index)
     siblings(0)
     tile([(0, 3)], both(0))
+    relay(0, (3, 4), (5, 6), (7, 4, 5, 6), (3, 8))
     siblings(1, 2)
     own_tile(both(0, 1))
-    relay(0, (3, 4), (5, 6), (7, 4, 5, 6), (3, 8))
     tile([(0, 3)], both(1, 2))
     relay(1, (3, 4), (5, 6), (7, 4, 5, 6), (3, 8))
-    for index in (4, 5, 6, 7):
+    for index in (4, 5):
         turn(index)
     tile([(4, 2)], both(0, 1, 2))
+    relay(0, (5, 6), (7, 8), (3, 8), ())
     old_first()
     siblings(3, 4)
-    relay(0, (5, 6), (7, 8), (3, 8), ())
     tile([(0, 2), (4, 2)], both(3, 4))
-    own_tile(both(2))
     relay(1, (5, 6), (), (3, 8), ())
-    for index in (3, 8):
-        turn(index)
+    turn(3)
     tile([(3, 1)], both(0, 1, 2))
     hand_b(2)
     tile([(2, 2)], both(3, 4))
     hand_b(4)
-    siblings(5, 6)
-    tile([(0, 2), (4, 2)], both(5, 6))
     for index in (7, 8):
         z_copy(index, z_part(index, 0)).wait_recv()
     c_copy(7).start()
+    siblings(5, 6)
+    tile([(0, 2), (4, 2)], both(5, 6))
     old_second()
+    turn(8)
     tile([(8, 1)], both(1, 3))
     siblings(7)
     tile([(0, 6)], both(7))
+    turn(6)
+    turn(7)
     hand_a(4, 5, 0, 1)
     tile([(8, 1)], both(5) + [mine, 14 + mine])
     hand_a(8)
@@ -368,7 +370,7 @@
     tile([(6, 2)], both(1, 3))
     hand_a(6, 7)
     hand_b(3, 1)
-    own_tile(both(3, 4))
+    own_tile(both(2, 3, 4))
     own_tile(both(5, 6, 7))
     hand_a(own)
 
@@ -381,8 +383,6 @@
     curv[0] = jnp.concatenate([pack(held + held.T), empty], axis=1)
     start_stage(curv_copies, 0)
 
-    rr = unpack(finish_stage(old_copies, old, old_in, 1), 0)
-    rr_inv = inverse(rr)
     product = part_a[own] + part_b[0] + ridge_weight * way
     for slot in (4, 5, 8, 9, 14, 15, 1, 10, 11, 12, 13):
         b_copy(slot).wait_recv()
@@ -399,6 +399,8 @@
     start_stage(gram_copies, 0)
     curv[1] = finish_stage(curv_copies, curv, curv_in, 0)
     start_stage(curv_copies, 1)
+    rr = unpack(finish_stage(old_copies, old, old_in, 1), 0)
+    rr_inv = inverse(rr)
     gram[1] = finish_stage(gram_copies, gram, gram_in, 0)
     start_stage(gram_copies, 1)
 

time: 65.3 us -> 63.8 us (0.977)
  Pallas kernels: 63.1 us -> 61.6 us
    pallas_call x1, Pallas kernels: 63.1 us -> 61.6 us  [shards(): pl.pallas_call(kernel, out_shape=jax.ShapeDtypeStruct((3 * rubrics, point...]
where the time goes in v5:
time: 63.8 us; the launch traced here: 63.7 us
  Pallas kernels  61.6 us (97%)
  local copies, waits for them, and re-layouts  1.37 us (2%)
  between operations  0.64 us (1%)
    pallas_call x1, Pallas kernels, shards(): pl.pallas_call(kernel, out_shape=jax.ShapeDtypeStruct((3 * rubrics, point...  61.6 us
    slice x1, local copies, waits for them, and re-layouts, shards(): return (stacked[0:16], stacked[16:32], stacked[32:48])  1.37 us

profile of v5, /device:TPU:1, one launch (start us, length us, event | category | flops | bytes accessed | tf_op | source)
XLA Modules:
  0.0 63.7 jit_solution(3626285890435846096)
XLA Ops:
  0.6 61.6 %iteration.1 = f32[48,256]{1,0:T(8,128)} custom-call(bf16[384,256]{1,0:T(8,128)(2,1)} %e_hbm.1, f32[16,256]{1,0:T(8,128)} %sol_hbm.1, f32[16,256]{1,0:T(8,128)} %res_hbm.1, f32[16,256]{1,0:T(8,128)} %dir_hbm.1), custom_call_target="tpu_custom_call" | custom-call | flops 20000000000 | bytes 1000000 | tf_op jit(solution)/shard_map/iteration/pallas_call | solution.py:438
  62.3 1.4 %fusion = (f32[16,256]{1,0:T(8,128)}, f32[16,256]{1,0:T(8,128)}, f32[16,256]{1,0:T(8,128)}) fusion(f32[48,256]{1,0:T(8,128)} %iteration.1), kind=kLoop, calls=%fused_computation | loop fusion | bytes 98304 | tf_op jit(solution)/shard_map/slice | solution.py:475

commit v6 on v5

--- a/solution.py
+++ b/solution.py
@@ -401,22 +401,6 @@
     start_stage(curv_copies, 1)
     rr = unpack(finish_stage(old_copies, old, old_in, 1), 0)
     rr_inv = inverse(rr)
-    gram[1] = finish_stage(gram_copies, gram, gram_in, 0)
-    start_stage(gram_copies, 1)
-
-    curvature_inv = inverse(unpack(finish_stage(curv_copies, curv, curv_in, 1), 0))
-    alpha_t = nn(rr, curvature_inv)
-    turned = nn(jnp.concatenate([curvature_inv, rr_inv], axis=0), way)
-    residual_next = rest - nn(alpha_t, product)
-    out[16:32] = residual_next
-    out[0:16] = sol_ref[...] + nn(alpha_t, way)
-    moved = residual_next + way
-
-    total = finish_stage(gram_copies, gram, gram_in, 1)
-    pr, pp = unpack(total, 0), unpack(total, 32)
-    inner = nn(jnp.concatenate([pp, -pr], axis=1), turned)
-    out[32:48] = moved + nn(alpha_t, inner) - nn(pr.T, turned[0:16])
-
     for index in others:
         pa_copy(index).wait_send()
         for part in (0, 1):
@@ -428,7 +412,26 @@
         c_copy(slot).wait_send()
     for slot in range(1, 16):
         b_copy(slot).wait_send()
-    for copy in old_copies + gram_copies + curv_copies:
+    for copy in old_copies:
+        copy.wait_send()
+    gram[1] = finish_stage(gram_copies, gram, gram_in, 0)
+    start_stage(gram_copies, 1)
+
+    curvature_inv = inverse(unpack(finish_stage(curv_copies, curv, curv_in, 1), 0))
+    alpha_t = nn(rr, curvature_inv)
+    turned = nn(jnp.concatenate([curvature_inv, rr_inv], axis=0), way)
+    residual_next = rest - nn(alpha_t, product)
+    out[16:32] = residual_next
+    out[0:16] = sol_ref[...] + nn(alpha_t, way)
+    moved = residual_next + way
+
+    for copy in curv_copies + gram_copies[:15]:
+        copy.wait_send()
+    total = finish_stage(gram_copies, gram, gram_in, 1)
+    pr, pp = unpack(total, 0), unpack(total, 32)
+    inner = nn(jnp.concatenate([pp, -pr], axis=1), turned)
+    out[32:48] = moved + nn(alpha_t, inner) - nn(pr.T, turned[0:16])
+    for copy in gram_copies[15:]:
         copy.wait_send()
 
 

time: 63.8 us -> 63.7 us (level)
  no operation moved by 1% of the time
where the time goes in v6:
time: 63.7 us; the launch traced here: 63.5 us
  Pallas kernels  61.5 us (97%)
  local copies, waits for them, and re-layouts  1.37 us (2%)
  between operations  0.64 us (1%)
    pallas_call x1, Pallas kernels, shards(): pl.pallas_call(kernel, out_shape=jax.ShapeDtypeStruct((3 * rubrics, point...  61.5 us
    slice x1, local copies, waits for them, and re-layouts, shards(): return (stacked[0:16], stacked[16:32], stacked[32:48])  1.37 us

profile of v6, /device:TPU:1, one launch (start us, length us, event | category | flops | bytes accessed | tf_op | source)
XLA Modules:
  0.0 63.5 jit_solution(7778031483270877199)
XLA Ops:
  0.6 61.5 %iteration.1 = f32[48,256]{1,0:T(8,128)} custom-call(bf16[384,256]{1,0:T(8,128)(2,1)} %e_hbm.1, f32[16,256]{1,0:T(8,128)} %sol_hbm.1, f32[16,256]{1,0:T(8,128)} %res_hbm.1, f32[16,256]{1,0:T(8,128)} %dir_hbm.1), custom_call_target="tpu_custom_call" | custom-call | flops 20000000000 | bytes 1000000 | tf_op jit(solution)/shard_map/iteration/pallas_call | solution.py:441
  62.1 1.4 %fusion = (f32[16,256]{1,0:T(8,128)}, f32[16,256]{1,0:T(8,128)}, f32[16,256]{1,0:T(8,128)}) fusion(f32[48,256]{1,0:T(8,128)} %iteration.1), kind=kLoop, calls=%fused_computation | loop fusion | bytes 98304 | tf_op jit(solution)/shard_map/slice | solution.py:478
